TPU v7x, 256 devices: a whole 4x4x8 slice. The times are simulated.
256 devices in a mesh: dp: 8 (over x, core), proto: 32 (over y, z).
Axes of the slice: x: 4, y: 4, z: 8, core: 2. Of those that a mesh axis runs over, the one named last changes fastest.
Arguments:
- first_view_embed: bfloat16 [8192, 512], P(('dp', 'proto')), may hold values from -40 to 40
- second_view_embed: bfloat16 [8192, 512], P(('dp', 'proto')), may hold values from -40 to 40
- prototypes: float32 [65536, 512], P(('dp', 'proto')), may hold values from -12 to 12
- pairing: int32 [8192], P('dp'), may hold values from 0 to 1023, as said below
Outputs:
- proto_grad: float32 [65536, 512], P(('dp', 'proto'))
- mean_loss: float32 [], replicated
Inputs may be any that keep to these rules, and one draw needn't show every extreme that they name: `pairing`: within each aligned block of 1024 frames the entries are a permutation of 0 to 1023.
All inputs are finite; a program needn't handle non-finite values.
Results may differ from a plain program's by a relative error of at most 0.015.
Values may be sent and summed in bfloat16 or wider, within the bound.
A program may use at most 128 MiB of HBM per device.

v0:
```python
import math

import jax
import jax.numpy as jnp
from jax import lax
from jax.sharding import PartitionSpec as P

ITERS = 3


MIN_MASS_BOUND = 0.05
SOFT_TEMP = 0.1
NORM_EPS = 1e-06


def unit_rows(matrix):
    widened = matrix.astype(jnp.float32)
    return (
        widened * lax.rsqrt(jnp.sum(widened * widened, axis=-1, keepdims=True) + NORM_EPS)
    ).astype(jnp.bfloat16)


def normalize_cluster_axis(optimal_transport_solver, sample_factor):
    column_part = jnp.einsum(
        "gq,gqw->gw", sample_factor, optimal_transport_solver, precision=lax.Precision.HIGHEST
    )
    cluster_factor = 1.0 / lax.psum(column_part, "dp")
    sample_slice = jnp.einsum(
        "wfy,wy->wf", optimal_transport_solver, cluster_factor, precision=lax.Precision.HIGHEST
    )
    return (cluster_factor, sample_slice)


def row_pass(sample_slice):
    return 1.0 / lax.psum(sample_slice, "proto")


def local(first_view_embed, second_view_embed, prototypes, pairing):
    unit_protos = unit_rows(prototypes)
    stacked = jnp.stack([unit_rows(first_view_embed), unit_rows(second_view_embed)])
    gathered = lax.all_gather(stacked, "proto", axis=1, tiled=True)
    partner = jnp.take(gathered[1], pairing, axis=0)
    both_views = jnp.stack([gathered[0], partner])
    centroid_similarity = jnp.einsum(
        "vbd,kd->vbk",
        both_views,
        lax.all_gather(unit_protos, "dp", axis=0, tiled=True),
        preferred_element_type=jnp.float32,
    )
    optimal_transport_solver = jnp.exp(centroid_similarity / MIN_MASS_BOUND)
    soft_exp = jnp.exp(centroid_similarity / SOFT_TEMP)
    soft_local = jnp.sum(soft_exp, axis=2)
    frame_count = centroid_similarity.shape[1]
    sample_factor = jnp.ones((2, frame_count), jnp.float32)
    cluster_factor, sample_slice = normalize_cluster_axis(optimal_transport_solver, sample_factor)
    sample_factor = row_pass(sample_slice)
    soft_total = lax.psum(soft_local, "proto")
    for sweep_index in range(1, ITERS):
        cluster_factor, sample_slice = normalize_cluster_axis(
            optimal_transport_solver, sample_factor
        )
        sample_factor = row_pass(sample_slice)
    code_targets = sample_factor[:, :, None] * optimal_transport_solver * cluster_factor[:, None, :]
    swapped = code_targets[::-1]
    predicted = soft_exp / soft_total[:, :, None]
    log_total = jnp.log(soft_total)
    loss_part = jnp.sum(swapped * (log_total[:, :, None] - centroid_similarity / SOFT_TEMP))
    frames_all = frame_count * lax.axis_size("dp")
    protos_all = centroid_similarity.shape[2] * lax.axis_size("proto")
    mean_loss = lax.psum(loss_part, ("dp", "proto")) / (2.0 * frames_all)
    grad_scale = protos_all / (SOFT_TEMP * math.sqrt(2.0 * frames_all))
    weights = ((predicted - swapped) * grad_scale).astype(jnp.bfloat16)
    proto_grad = lax.psum_scatter(
        jnp.einsum("vbk,vbd->kd", weights, both_views, preferred_element_type=jnp.float32).astype(
            jnp.bfloat16
        ),
        "dp",
        scatter_dimension=0,
        tiled=True,
    ).astype(jnp.float32)
    return (proto_grad, mean_loss)


def solution(mesh):
    return jax.shard_map(
        local,
        mesh=mesh,
        in_specs=(
            P(("dp", "proto"), None),
            P(("dp", "proto"), None),
            P(("dp", "proto"), None),
            P("dp"),
        ),
        out_specs=(P(("dp", "proto"), None), P()),
        check_vma=False,
    )
```

profile of v0, /device:TPU:1, one launch (start us, length us, event | category | flops | bytes accessed | tf_op | source)
XLA Modules:
  0.0 692.2 jit_solution(18348962776330645839)
XLA Ops:
  7.2 0.0 all-gather.3.cloned.1.call-start
  7.2 0.9 fusion.8
  8.1 0.9 fusion.10
  9.0 0.9 fusion.12
  9.8 0.6 pad_maximum_fusion.3
  10.5 0.0 all-gather.3.cloned.1.call-update
  10.5 0.0 all-gather.5.cloned.1.call-start
  10.6 1.2 multiply_reduce_fusion.1
  11.7 1.9 multiply_convert_fusion.1
  13.6 0.0 all-gather.5.cloned.1.call-update
  13.6 0.0 reduce-scatter.2.cloned.1.call-start
  13.7 0.7 compare_and_fusion
  14.4 0.7 fusion.20
  15.0 73.5 %all-gather.3.cloned.1.call-done = bf16[2,1024,512]{2,1,0:T(8,128)(2,1)} async-done(((bf16[2,32,512]{2,1,0:T(8,128)(2,1)}), bf16[2,1024,512]{2,1,0:T(8,128)(2,1)}) %all-gather.3.cloned.1.call-update) | async-done | bytes 2097168 | tf_op jit(solution)/shard_map/all_gather | solution.py:41
  88.5 1.7 fusion.30
  90.2 4.0 gather_fusion
  94.2 0.2 bitcast_select_fusion
  94.4 25.8 %all-gather.5.cloned.1.call-done = bf16[2048,512]{1,0:T(8,128)(2,1)} async-done(((bf16[256,512]{1,0:T(8,128)(2,1)}), bf16[2048,512]{1,0:T(8,128)(2,1)}) %all-gather.5.cloned.1.call-update) | async-done | bytes 2097168 | tf_op jit(solution)/shard_map/all_gather | solution.py:47
  120.2 6.8 exponential_reduce_fusion
  127.0 0.0 copy-start
  127.0 5.7 copy-done
  132.7 9.5 %fusion.5 = f32[2,1,2048]{2,1,0:T(1,128)S(1)} fusion(f32[2,1024,2048]{2,1,0:T(8,128)S(1)} %get-tuple-element.9), kind=kOutput, calls=%fused_computation.11 | convolution fusion | flops 54525952 | bytes 16793600 | tf_op jit(solution)/shard_map/gq,gqw->gw/dot_general | solution.py:24
  142.3 21.7 %psum.57 = f32[2,2048]{1,0:T(2,128)S(1)} all-reduce(f32[2,2048]{1,0:T(2,128)S(1)} %bitcast.44), channel_id=1, replica_groups=mesh['dp'=8,'proto'=32] {'dp'}, use_global_device_ids=true, to_apply=%region_5.6 | all-reduce | flops 4096 | bytes 32768 | tf_op jit(solution)/shard_map/psum | solution.py:27
  164.0 19.1 %fusion.4 = f32[2,1,1024]{2,1,0:T(1,128)S(1)} fusion(f32[2,1024,2048]{2,1,0:T(8,128)} %copy-done, f32[2,2048,1]{1,0,2:T(2,128)S(1)} %divide_bitcast_fusion.1), kind=kOutput, calls=%fused_computation.10 | convolution fusion | flops 54525952 | bytes 16801792 | tf_op jit(solution)/shard_map/wfy,wy->wf/dot_general | solution.py:28
  183.1 62.1 %psum.58 = f32[2,1024]{1,0:T(2,128)S(1)} all-reduce(f32[2,1024]{1,0:T(2,128)S(1)} %bitcast.48), channel_id=1, replica_groups=mesh['dp'=8,'proto'=32] {'proto'}, use_global_device_ids=true, to_apply=%region_6.7 | all-reduce | flops 2048 | bytes 16384 | tf_op jit(solution)/shard_map/psum | solution.py:35
  245.3 13.1 %fusion.3 = f32[2,1,2048]{2,1,0:T(1,128)S(1)} fusion(f32[2,1024,2048]{2,1,0:T(8,128)} %copy-done, f32[2,1024,1]{1,0,2:T(2,128)S(1)} %divide_bitcast_fusion.3), kind=kOutput, calls=%fused_computation.9 | convolution fusion | flops 54525952 | bytes 16801792 | tf_op jit(solution)/shard_map/gq,gqw->gw/dot_general | solution.py:24
  258.4 37.6 %psum.59 = f32[2,2048]{1,0:T(2,128)S(1)} all-reduce(f32[2,2048]{1,0:T(2,128)S(1)} %bitcast.45), channel_id=1, replica_groups=mesh['dp'=8,'proto'=32] {'dp'}, use_global_device_ids=true, to_apply=%region_7.8 | all-reduce | flops 4096 | bytes 32768 | tf_op jit(solution)/shard_map/psum | solution.py:27
  296.0 19.1 %fusion.2 = f32[2,1,1024]{2,1,0:T(1,128)S(1)} fusion(f32[2,1024,2048]{2,1,0:T(8,128)} %copy-done, f32[2,2048,1]{1,0,2:T(2,128)S(1)} %divide_bitcast_fusion), kind=kOutput, calls=%fused_computation.8 | convolution fusion | flops 54525952 | bytes 16801792 | tf_op jit(solution)/shard_map/wfy,wy->wf/dot_general | solution.py:28
  315.1 56.7 %psum.60 = f32[2,1024]{1,0:T(2,128)S(1)} all-reduce(f32[2,1024]{1,0:T(2,128)S(1)} %bitcast.49), channel_id=1, replica_groups=mesh['dp'=8,'proto'=32] {'proto'}, use_global_device_ids=true, to_apply=%region_8.9 | all-reduce | flops 2048 | bytes 16384 | tf_op jit(solution)/shard_map/psum | solution.py:35
  371.9 13.3 %fusion.1 = f32[2,1,2048]{2,1,0:T(1,128)S(1)} fusion(f32[2,1024,2048]{2,1,0:T(8,128)} %copy-done, f32[2,1024,1]{1,0,2:T(2,128)S(1)} %divide_bitcast_fusion.2), kind=kOutput, calls=%fused_computation.7 | convolution fusion | flops 54525952 | bytes 16801792 | tf_op jit(solution)/shard_map/gq,gqw->gw/dot_general | solution.py:24
  385.2 37.5 %psum.61 = f32[2,2048]{1,0:T(2,128)S(1)} all-reduce(f32[2,2048]{1,0:T(2,128)S(1)} %bitcast.46), channel_id=1, replica_groups=mesh['dp'=8,'proto'=32] {'dp'}, use_global_device_ids=true, to_apply=%region_9.10 | all-reduce | flops 4096 | bytes 32768 | tf_op jit(solution)/shard_map/psum | solution.py:27
  422.7 19.1 %fusion = f32[2,1,1024]{2,1,0:T(1,128)S(1)} fusion(f32[2,1024,2048]{2,1,0:T(8,128)} %copy-done, f32[2,2048,1]{1,0,2:T(2,128)S(1)} %fusion.32), kind=kOutput, calls=%fused_computation.6 | convolution fusion | flops 54525952 | bytes 16801792 | tf_op jit(solution)/shard_map/wfy,wy->wf/dot_general | solution.py:28
  441.8 112.2 %all-reduce = (f32[2,1024]{1,0:T(2,128)S(1)}, f32[2,1024]{1,0:T(2,128)S(1)}) all-reduce(f32[2,1024]{1,0:T(2,128)S(1)} %bitcast.47, f32[2,1024]{1,0:T(2,128)S(1)} %get-tuple-element.8), channel_id=1, replica_groups=mesh['dp'=8,'proto'=32] {'proto'}, use_global_device_ids=true, to_apply=%region_10.11 | all-reduce | flops 4096 | bytes 32768 | tf_op jit(solution)/shard_map/psum | solution.py:35
  554.1 7.3 %multiply_multiply_fusion = f32[2,1024,2048]{2,1,0:T(8,128)S(1)} fusion(f32[2,2048]{1,0:T(2,128)S(1)} %broadcast_divide_fusion, f32[2,1024]{1,0:T(2,128)S(1)} %broadcast_divide_fusion.1, f32[2,1024,2048]{2,1,0:T(8,128)} %copy-done), kind=kLoop, calls=%fused_computation.3 | loop fusion | flops 12582912 | bytes 33579008 | tf_op jit(solution)/shard_map/mul | solution.py:63
  561.4 12.5 %multiply_reduce_fusion = (f32[]{:T(128)}, bf16[2,1024,2048]{2,1,0:T(8,128)(2,1)S(1)}) fusion(f32[2,1024,2048]{2,1,0:T(8,128)S(1)} %multiply_multiply_fusion, f32[2,1024,2048]{2,1,0:T(8,128)} %copy-done, f32[2,1024]{1,0:T(2,128)S(1)} %log.3, f32[2,1024]{1,0:T(2,128)S(1)} %get-tuple-element.3), kind=kLoop, calls=%fused_computation.1 | loop fusion | flops 33554432 | bytes 41959428 | tf_op jit(solution)/shard_map/reduce_sum | solution.py:67
  573.9 6.3 bitcast_convert_fusion
  580.2 0.0 reduce-scatter.2.cloned.1.call-update
  580.3 101.7 %psum.63 = f32[]{:T(128)} all-reduce(f32[]{:T(128)} %get-tuple-element.4), channel_id=1, replica_groups=mesh['dp'=8,'proto'=32] {'dp','proto'}, use_global_device_ids=true, to_apply=%region_13.14 | all-reduce | flops 1 | bytes 8 | tf_op jit(solution)/shard_map/psum | solution.py:70
  682.6 0.0 reduce-scatter.2.cloned.1.call-done
  682.6 1.8 convert_element_type.31
  (17 shorter events, 0.2 us)
Async XLA Ops:
  7.2 81.4 %all-gather.3.cloned.1.call-start = ((), (), s32[]{:S(2)}) async-start(), calls=%async_computation.1 | async-start | bytes 2162688 | tf_op jit(solution)/shard_map/all_gather | solution.py:41
  10.5 109.7 %all-gather.5.cloned.1.call-start = ((), (), s32[]{:S(2)}) async-start(), calls=%async_computation.2 | async-start | bytes 2359296 | tf_op jit(solution)/shard_map/all_gather | solution.py:47
  13.6 669.0 %reduce-scatter.2.cloned.1.call-start = ((), (), s32[]{:S(2)}) async-start(), calls=%async_computation.3 | async-start | bytes 2359296 | tf_op jit(solution)/shard_map/reduce_scatter | solution.py:73
  127.0 5.7 copy-start
Sparse Core Ops, SparseCore 0:
  10.6 77.8 all-gather.2
  91.0 29.1 all-gather.4
  580.4 55.1 reduce-scatter.1
where the time goes:
time: 702 us; the launch traced here: 692 us
  blocking collectives  430 us (61%)
  matrix products  106 us (15%)
  waiting for transfers between devices  99.4 us (14%)
  other arithmetic  29.6 us (4%)
  between operations  15.9 us (2%)
  local copies, waits for them, and re-layouts  11.4 us (2%)
    psum x3, blocking collectives, row_pass(): return 1.0 / lax.psum(sample_slice, 'proto')  231 us
    psum x1, blocking collectives, local(): mean_loss = lax.psum(loss_part, ('dp', 'proto')) / (2.0 * frames_all)  102 us
    psum x3, blocking collectives, normalize_cluster_axis(): cluster_factor = 1.0 / lax.psum(column_part, 'dp')  96.8 us
    all_gather x1, waiting for transfers between devices, local(): gathered = lax.all_gather(stacked, 'proto', axis=1, tiled=True)  73.5 us
    dot_general x3, matrix products, normalize_cluster_axis(): jnp.einsum('wfy,wy->wf', optimal_transport_solver, cluster_factor, precis...  57.3 us
    dot_general x3, matrix products, normalize_cluster_axis(): jnp.einsum('gq,gqw->gw', sample_factor, optimal_transport_solver, precisi...  35.9 us
    all_gather x1, waiting for transfers between devices, local(): lax.all_gather(unit_protos, 'dp', axis=0, tiled=True)  25.8 us
  transfers between devices with their start and end apart: 3, of which 2 were waited for; matrix products, arithmetic and copies ran while one was open for 1% of the time, Pallas kernels for 0%

commit v1 on v0

v1 whole, which is shorter than its diff:
```python
import functools
import math

import jax
import jax.numpy as jnp
from jax import lax
from jax.experimental import pallas as pl
from jax.experimental.pallas import tpu as pltpu
from jax.sharding import PartitionSpec as P

ITERS = 3
SOFT_TEMP = 0.1
NORM_EPS = 1e-06
CORES = 2
DEPTH = 8

F32 = jnp.float32
BF16 = jnp.bfloat16
NT = (((1,), (1,)), ((), ()))
NN = (((1,), (0,)), ((), ()))


def unit_rows(matrix):
    widened = matrix.astype(F32)
    return (
        widened * lax.rsqrt(jnp.sum(widened * widened, axis=-1, keepdims=True) + NORM_EPS)
    ).astype(BF16)


def drain(ref, sem):
    pltpu.make_async_copy(ref, ref, sem).wait()


def rows_to_lanes(acc_ref, view, out_ref, rows):
    for b in range(rows // 128):
        block = acc_ref[view, b * 128 : (b + 1) * 128, :]
        out_ref[b : b + 1, :] = jnp.sum(block.T, axis=0, keepdims=True)


def lanes_to_rows(dense, out_ref, view, rows):
    for b in range(rows // 128):
        block = jnp.broadcast_to(dense[b : b + 1, :], (128, 128))
        out_ref[view, b * 128 : (b + 1) * 128, :] = block.T


def kernel(
    sizes,
    first_ref,
    second_ref,
    protos_ref,
    pair_ref,
    grad_ref,
    loss_ref,
    v_ref,
    partner_ref,
    p_ref,
    onehot_ref,
    ut_ref,
    e_ref,
    acc_ref,
    soft_acc_ref,
    rb_ref,
    sb_ref,
    cs_ref,
    c_ref,
    r_ref,
    row_ref,
    t_ref,
    w_ref,
    g_ref,
    dp_src,
    dp_buf,
    y_src,
    y_buf,
    z_src,
    z_buf,
    soft_src,
    soft_ybuf,
    soft_mid,
    soft_zbuf,
    loss_src,
    loss_ybuf,
    loss_zbuf,
    loss_xbuf,
    ss_ref,
    sr_ref,
    xs_ref,
    xr_ref,
    ay_s,
    ay_r,
    az_s,
    az_r,
    bz_s,
    bz_r,
    by_s,
    by_r,
    px_s,
    px_r,
    ps_s,
    ps_r,
    dp_s,
    dp_r,
    y_s,
    y_r,
    z_s,
    z_r,
    soft_s,
    soft_r,
    loss_s,
    loss_r,
    ss_s,
    ss_r,
    xs_s,
    xs_r,
):
    nx, ny, nz, fr, width, pr = sizes
    frames = fr * ny * nz
    group = fr * ny
    protos = pr * nx * CORES
    ptiles = protos // 128
    tiles_pr = pr // 128
    fdense = frames // 128
    grad_scale = protos * ny * nz / (SOFT_TEMP * math.sqrt(2.0 * frames * nx * CORES))

    dp, pi = lax.axis_index("dp"), lax.axis_index("proto")
    x, core = dp // CORES, dp % CORES
    y, z = pi // nz, pi % nz

    def at(dx=0, dc=0, dy=0, dz=0):
        return {
            "dp": lax.rem(x + dx, nx) * CORES + lax.rem(core + dc, CORES),
            "proto": lax.rem(y + dy, ny) * nz + lax.rem(z + dz, nz),
        }

    def send(src, dst, ssem, rsem, device):
        pltpu.make_async_remote_copy(
            src_ref=src,
            dst_ref=dst,
            send_sem=ssem,
            recv_sem=rsem,
            device_id=device,
            device_id_type=pl.DeviceIdType.MESH,
        ).start()

    sib = at(dc=1)
    xs = [at(dx=d) for d in range(1, nx)]
    ys = [at(dy=d) for d in range(1, ny)]
    zs = [at(dz=d) for d in range(1, nz)]
    dps = [at(dx=d, dc=e) for d in range(nx) for e in range(CORES) if d or e]

    barrier = pltpu.get_barrier_semaphore()
    for device in dps + ys + zs:
        pl.semaphore_signal(
            barrier, inc=1, device_id=device, device_id_type=pl.DeviceIdType.MESH
        )
    v_ref[0, z, y] = unit_rows(first_ref[...])
    v_ref[1, z, y] = unit_rows(second_ref[...])
    p_ref[dp] = unit_rows(protos_ref[...])
    pl.semaphore_wait(barrier, len(dps) + len(ys) + len(zs))

    for device in ys:
        send(v_ref.at[0, z, y], v_ref.at[0, z, y], ay_s, ay_r, device)
    for j, device in enumerate(xs):
        send(p_ref.at[dp], p_ref.at[dp], px_s, px_r.at[j], device)
    z_order = []
    for d in range(1, nz // 2 + 1):
        z_order.append(d)
        if nz - d != d:
            z_order.append(nz - d)
    for d in z_order:
        send(v_ref.at[1, z, y], v_ref.at[1, z, y], bz_s, bz_r.at[d - 1], zs[d - 1])
    send(p_ref.at[dp], p_ref.at[dp], ps_s, ps_r, sib)
    for device in ys:
        send(v_ref.at[1, z, y], v_ref.at[1, z, y], by_s, by_r, device)

    pair = pair_ref[...]
    where = (pair % (nz * fr) // fr) * group + (pair // (nz * fr)) * fr + pair % fr
    where = where.astype(F32)
    for b in range(fdense):
        column = jnp.broadcast_to(where[b : b + 1, :], (128, 128)).T
        for t in range(fdense):
            lane = (lax.broadcasted_iota(jnp.int32, (128, 128), 1) + t * 128).astype(F32)
            block = jnp.where(column == lane, 1.0, 0.0).astype(BF16)
            for q in range(128 // fr):
                natural = b * 128 + q * fr
                row = (natural % (nz * fr) // fr) * group + natural // (nz * fr) * fr
                onehot_ref[row : row + fr, t * 128 : (t + 1) * 128] = block[
                    q * fr : (q + 1) * fr, :
                ]
    cs_ref[...] = jnp.zeros_like(cs_ref)
    soft_acc_ref[...] = jnp.zeros_like(soft_acc_ref)

    def wait_frames_z(d):
        zb = lax.rem(z + nz - d, nz)
        drain(v_ref.at[1, zb, y], bz_r.at[d - 1])
        for device in ys:
            send(v_ref.at[1, zb, y], v_ref.at[1, zb, y], by_s, by_r, device)

    half = ny // 2

    def ring_blocks(step):
        up = lax.rem(z + nz - (step - 1), nz)
        down = lax.rem(z + step - 1, nz)
        if step < nz // 2:
            return v_ref.at[0, up], v_ref.at[0, down]
        return v_ref.at[0, up, pl.ds(0, half)], v_ref.at[0, down, pl.ds(half, half)]

    def ring_send(step):
        up, down = ring_blocks(step)
        send(up, up, az_s.at[0, step - 1], az_r.at[0, step - 1], zs[0])
        send(down, down, az_s.at[1, step - 1], az_r.at[1, step - 1], zs[nz - 2])

    def ring_wait(step):
        up, down = ring_blocks(step)
        drain(up, az_r.at[0, step - 1])
        drain(down, az_r.at[1, step - 1])

    def wait_protos_x(j):
        owner = lax.rem(x + nx - (j + 1), nx) * CORES + core
        drain(p_ref.at[owner], px_r.at[j])
        send(p_ref.at[owner], p_ref.at[owner], ps_s, ps_r, sib)

    def first_pass(view, rows, row, block):
        count = block.shape[0]

        def step(j, carry):
            cols = pl.ds(pl.multiple_of(j * pr, pr), pr)
            scores = lax.dot_general(block, p_ref[j], NT, preferred_element_type=F32)
            e = jnp.exp(scores / SOFT_TEMP)
            e_ref[view, rows, cols] = e
            total = e[:, 0:128]
            for t in range(1, tiles_pr):
                total = total + e[:, t * 128 : (t + 1) * 128]
            soft_acc_ref[view, rows, :] += total
            cs_ref[view, :, cols] += jnp.sum((e * e).reshape(count // 8, 8, pr), axis=0)
            return carry

        lax.fori_loop(0, nx * CORES, step, 0)

    def zero_block(zb):
        rows = pl.ds(pl.multiple_of(zb * group, group), group)
        first_pass(0, rows, zb, v_ref[0, zb].reshape(group, width))

    drain(v_ref.at[0, 0, pl.ds(0, ny - 1)], ay_r)
    ring_send(1)
    near = z_order[: (nz - 1) // 2]
    far = z_order[(nz - 1) // 2 :]
    for d in near:
        wait_frames_z(d)
    if nz // 2 > 1:
        ring_wait(1)
        ring_send(2)
    for d in far:
        wait_frames_z(d)
    x_order = sorted(range(nx - 1), key=lambda j: min(j + 1, nx - j - 1))
    for j in x_order[:-1]:
        wait_protos_x(j)
    for step in range(3, nz // 2):
        ring_wait(step - 1)
        ring_send(step)
    wait_protos_x(x_order[-1])
    drain(p_ref.at[pl.ds(0, nx)], ps_r)
    if nz // 2 > 2:
        ring_wait(nz // 2 - 1)
        ring_send(nz // 2)
    drain(v_ref.at[1, :, pl.ds(0, ny - 1)], by_r)

    chunk = min(256, frames)

    def permute(i, carry):
        rows = pl.ds(pl.multiple_of(i * chunk, chunk), chunk)
        partner_ref[rows, :] = lax.dot_general(
            onehot_ref[rows, :],
            v_ref[1].reshape(frames, width),
            NN,
            preferred_element_type=F32,
        ).astype(BF16)
        first_pass(1, rows, i, partner_ref[rows, :])
        return carry

    lax.fori_loop(0, frames // chunk, permute, 0)

    def dp_start(view, it, source):
        slot = it % 2
        if it >= 2:
            drain(dp_buf.at[view, slot], dp_s.at[view, slot])
        dp_src[view, slot] = source
        for j, device in enumerate(dps):
            send(
                dp_src.at[view, slot],
                dp_buf.at[view, slot, j],
                dp_s.at[view, slot],
                dp_r.at[view, slot],
                device,
            )

    def dp_wait(view, it):
        slot = it % 2
        drain(dp_buf.at[view, slot], dp_r.at[view, slot])
        total = dp_src[view, slot]
        for j in range(len(dps)):
            total = total + dp_buf[view, slot, j]
        return total

    def y_start(view, it):
        slot = it % 2
        if it >= 2:
            drain(y_buf.at[view, slot], y_s.at[view, slot])
        y_src[view, slot] = row_ref[view]
        for j, device in enumerate(ys):
            send(
                y_src.at[view, slot],
                y_buf.at[view, slot, j],
                y_s.at[view, slot],
                y_r.at[view, slot],
                device,
            )

    def y_wait(view, it):
        slot = it % 2
        drain(y_buf.at[view, slot], y_r.at[view, slot])
        total = y_src[view, slot]
        for j in range(len(ys)):
            total = total + y_buf[view, slot, j]
        if it >= 2:
            drain(z_buf.at[view, slot], z_s.at[view, slot])
        z_src[view, slot] = total
        for j, device in enumerate(zs):
            send(
                z_src.at[view, slot],
                z_buf.at[view, slot, j],
                z_s.at[view, slot],
                z_r.at[view, slot],
                device,
            )

    def z_wait(view, it):
        slot = it % 2
        drain(z_buf.at[view, slot], z_r.at[view, slot])
        total = z_src[view, slot]
        for j in range(len(zs)):
            total = total + z_buf[view, slot, j]
        return total

    def column_totals(view):
        parts = [
            jnp.sum(cs_ref[view, :, t * 128 : (t + 1) * 128], axis=0, keepdims=True)
            for t in range(ptiles)
        ]
        return jnp.concatenate(parts, axis=0)

    def frame_sums(view):
        def step(i, carry):
            rows = pl.ds(pl.multiple_of(i * 64, 64), 64)
            total = jnp.zeros((64, 128), F32)
            for t in range(ptiles):
                e = e_ref[view, rows, t * 128 : (t + 1) * 128]
                total = total + (e * e) * c_ref[view, t : t + 1, :]
            acc_ref[view, rows, :] = total
            return carry

        lax.fori_loop(0, frames // 64, step, 0)
        rows_to_lanes(acc_ref, view, row_ref.at[view], frames)

    def proto_sums(view):
        def step(i, totals):
            rows = pl.ds(pl.multiple_of(i * 32, 32), 32)
            scale = rb_ref[view, rows, :]
            out = []
            for t in range(ptiles):
                e = e_ref[view, rows, t * 128 : (t + 1) * 128]
                out.append(
                    totals[t] + jnp.sum(((e * e) * scale).reshape(4, 8, 128), axis=0)
                )
            return tuple(out)

        totals = lax.fori_loop(
            0, frames // 32, step, tuple(jnp.zeros((8, 128), F32) for _ in range(ptiles))
        )
        for t in range(ptiles):
            cs_ref[view, :, t * 128 : (t + 1) * 128] = totals[t]

    dp_start(1, 0, column_totals(1))
    for d in range(nz // 2):
        zero_block(lax.rem(z + d, nz))
        if d:
            zero_block(lax.rem(z + nz - d, nz))
    ring_wait(nz // 2)
    zero_block(lax.rem(z + nz // 2, nz))
    dp_start(0, 0, column_totals(0))

    for view in range(2):
        rows_to_lanes(soft_acc_ref, view, soft_src.at[pl.ds(view * fdense, fdense)], frames)
    for j, device in enumerate(ys):
        send(soft_src, soft_ybuf.at[j], soft_s.at[0], soft_r.at[0], device)

    eye = jnp.where(
        lax.broadcasted_iota(jnp.int32, (width, width), 0)
        == lax.broadcasted_iota(jnp.int32, (width, width), 1),
        1.0,
        0.0,
    ).astype(BF16)

    def transpose_view(view):
        for i in range(frames // chunk):
            if view:
                block = partner_ref[i * chunk : (i + 1) * chunk, :]
            else:
                count = chunk // group
                block = v_ref[0, i * count : (i + 1) * count].reshape(chunk, width)
            ut_ref[view, :, i * chunk : (i + 1) * chunk] = lax.dot_general(
                eye, block, NT, preferred_element_type=F32
            ).astype(BF16)

    transpose_view(1)

    for it in range(ITERS):
        for view in (1, 0):
            c_ref[view] = 1.0 / dp_wait(view, it)
            frame_sums(view)
            y_start(view, it)
        if it == 0:
            transpose_view(0)
            drain(soft_ybuf, soft_r.at[0])
            total = soft_src[...]
            for j in range(len(ys)):
                total = total + soft_ybuf[j]
            soft_mid[...] = total
        for view in (1, 0):
            y_wait(view, it)
        if it == 0:
            for j, device in enumerate(zs):
                send(soft_mid, soft_zbuf.at[j], soft_s.at[1], soft_r.at[1], device)
        if it == 1:
            drain(soft_zbuf, soft_r.at[1])
            total = soft_mid[...]
            for j in range(len(zs)):
                total = total + soft_zbuf[j]
            soft_mid_total = total
            for view in range(2):
                dense = soft_mid_total[view * fdense : (view + 1) * fdense]
                lanes_to_rows(grad_scale / dense, sb_ref, view, frames)
                r_ref[2 + view] = jnp.log(dense)
        if it == ITERS - 1:
            def step(i, carry):
                rows = pl.ds(pl.multiple_of(i * 32, 32), 32)
                sums = [jnp.zeros((32, 128), F32), jnp.zeros((32, 128), F32)]
                for t in range(ptiles):
                    e = [e_ref[v, rows, t * 128 : (t + 1) * 128] for v in range(2)]
                    for v in range(2):
                        term = (e[v] * e[v]) * c_ref[v, t : t + 1, :]
                        sums[v] = sums[v] + term * jnp.log(e[1 - v])
                for v in range(2):
                    acc_ref[v, rows, :] = sums[v]
                return carry

            lax.fori_loop(0, frames // 32, step, 0)
            for v in range(2):
                rows_to_lanes(acc_ref, v, t_ref.at[v], frames)
        for view in (1, 0):
            r = 1.0 / z_wait(view, it)
            r_ref[view] = r
            if it < ITERS - 1:
                lanes_to_rows(r, rb_ref, view, frames)
                proto_sums(view)
                dp_start(view, it + 1, column_totals(view))
            else:
                lanes_to_rows(r * grad_scale, rb_ref, view, frames)

    loss = jnp.zeros((fdense, 128), F32)
    for v in range(2):
        loss = loss + r_ref[v] * (r_ref[3 - v] * row_ref[v] - t_ref[v])
    loss_src[0] = loss
    for j, device in enumerate(ys):
        send(loss_src.at[0], loss_ybuf.at[j], loss_s.at[0], loss_r.at[0], device)

    def loss_step(stage, buf, nextbuf, partners):
        drain(buf, loss_r.at[stage])
        total = loss_src[stage]
        for j in range(buf.shape[0]):
            total = total + buf[j]
        if nextbuf is None:
            return total
        loss_src[stage + 1] = total
        for j, device in enumerate(partners):
            send(
                loss_src.at[stage + 1],
                nextbuf.at[j],
                loss_s.at[stage + 1],
                loss_r.at[stage + 1],
                device,
            )
        return total

    def block_grad(owner, out):
        def weigh(i, carry):
            rows = pl.ds(pl.multiple_of(i * 64, 64), 64)
            for t in range(tiles_pr):
                tile = owner * tiles_pr + t
                cols = pl.ds(pl.multiple_of(tile * 128, 128), 128)
                e = [e_ref[v, rows, cols] for v in range(2)]
                assigned = [
                    (e[v] * e[v]) * (rb_ref[v, rows, :] * c_ref[v, pl.ds(tile, 1), :])
                    for v in range(2)
                ]
                for v in range(2):
                    w_ref[v, rows, t * 128 : (t + 1) * 128] = (
                        e[v] * sb_ref[v, rows, :] - assigned[1 - v]
                    ).astype(BF16)
            return carry

        lax.fori_loop(0, frames // 64, weigh, 0)
        mrows = min(256, width)
        for m in range(width // mrows):
            rows = slice(m * mrows, (m + 1) * mrows)
            total = lax.dot_general(
                ut_ref[0, rows, :], w_ref[0], NN, preferred_element_type=F32
            ) + lax.dot_general(
                ut_ref[1, rows, :], w_ref[1], NN, preferred_element_type=F32
            )
            out[rows, :] = total.astype(out.dtype)

    order = sorted(range(nx), key=lambda d: -min(d, nx - d))
    for k, d in enumerate(order):
        xt = lax.rem(x + d, nx)
        block_grad(xt * CORES + (1 - core), ss_ref.at[k])
        send(ss_ref.at[k], sr_ref.at[k], ss_s, ss_r.at[k], sib)
        block_grad(xt * CORES + core, g_ref)
        drain(sr_ref.at[k], ss_r.at[k])
        if d:
            xs_ref[d - 1] = (g_ref[...] + sr_ref[k].astype(F32)).astype(BF16)
            send(xs_ref.at[d - 1], xr_ref.at[d - 1], xs_s, xs_r, xs[d - 1])
        else:
            g_ref[...] = g_ref[...] + sr_ref[k].astype(F32)
        if k == 1:
            loss_step(0, loss_ybuf, loss_zbuf, zs)
    loss_step(1, loss_zbuf, loss_xbuf, dps)
    drain(xr_ref, xs_r)
    for i in range(width // 128):
        for t in range(tiles_pr):
            rows, cols = slice(i * 128, (i + 1) * 128), slice(t * 128, (t + 1) * 128)
            total = g_ref[rows, cols]
            for j in range(nx - 1):
                total = total + xr_ref[j, rows, cols].astype(F32)
            grad_ref[cols, rows] = total.T
    total = loss_step(2, loss_xbuf, None, None)
    loss_ref[0, 0] = jnp.sum(total) / (2.0 * frames * nx * CORES)

    drain(v_ref.at[0, 0, pl.ds(0, ny - 1)], ay_s)
    for step in range(1, nz // 2 + 1):
        up, down = ring_blocks(step)
        drain(up, az_s.at[0, step - 1])
        drain(down, az_s.at[1, step - 1])
    drain(v_ref.at[1, pl.ds(0, nz - 1), 0], bz_s)
    drain(v_ref.at[1, :, pl.ds(0, ny - 1)], by_s)
    drain(p_ref.at[pl.ds(0, nx - 1)], px_s)
    drain(p_ref.at[pl.ds(0, nx)], ps_s)
    for view in range(2):
        for slot in range(min(2, ITERS)):
            drain(dp_buf.at[view, slot], dp_s.at[view, slot])
            drain(y_buf.at[view, slot], y_s.at[view, slot])
            drain(z_buf.at[view, slot], z_s.at[view, slot])
    drain(soft_ybuf, soft_s.at[0])
    drain(soft_zbuf, soft_s.at[1])
    drain(loss_ybuf, loss_s.at[0])
    drain(loss_zbuf, loss_s.at[1])
    drain(loss_xbuf, loss_s.at[2])
    drain(sr_ref, ss_s)
    drain(xr_ref, xs_s)


def solution(mesh):
    ndp, nproto = mesh.shape["dp"], mesh.shape["proto"]
    nx, nz = ndp // CORES, DEPTH
    ny = nproto // nz

    def local(first, second, protos, pairing):
        fr, width = first.shape
        pr = protos.shape[0]
        frames = fr * nproto
        cols = pr * ndp
        fd = frames // 128
        ct = cols // 128
        sem = pltpu.SemaphoreType.DMA
        sizes = (nx, ny, nz, fr, width, pr)
        vmem = pltpu.VMEM
        grad, loss = pl.pallas_call(
            functools.partial(kernel, sizes),
            out_shape=(
                jax.ShapeDtypeStruct((pr, width), F32),
                jax.ShapeDtypeStruct((1, 1), F32),
            ),
            in_specs=[pl.BlockSpec(memory_space=pltpu.VMEM)] * 4,
            out_specs=(
                pl.BlockSpec(memory_space=pltpu.VMEM),
                pl.BlockSpec(memory_space=pltpu.SMEM),
            ),
            scratch_shapes=[
                vmem((2, nz, ny, fr, width), BF16),
                vmem((frames, width), BF16),
                vmem((ndp, pr, width), BF16),
                vmem((frames, frames), BF16),
                vmem((2, width, frames), BF16),
                vmem((2, frames, cols), F32),
                vmem((2, frames, 128), F32),
                vmem((2, frames, 128), F32),
                vmem((2, frames, 128), F32),
                vmem((2, frames, 128), F32),
                vmem((2, 8, cols), F32),
                vmem((2, ct, 128), F32),
                vmem((4, fd, 128), F32),
                vmem((2, fd, 128), F32),
                vmem((2, fd, 128), F32),
                vmem((2, frames, pr), BF16),
                vmem((width, pr), F32),
                vmem((2, 2, ct, 128), F32),
                vmem((2, 2, ndp - 1, ct, 128), F32),
                vmem((2, 2, fd, 128), F32),
                vmem((2, 2, ny - 1, fd, 128), F32),
                vmem((2, 2, fd, 128), F32),
                vmem((2, 2, nz - 1, fd, 128), F32),
                vmem((2 * fd, 128), F32),
                vmem((ny - 1, 2 * fd, 128), F32),
                vmem((2 * fd, 128), F32),
                vmem((nz - 1, 2 * fd, 128), F32),
                vmem((3, fd, 128), F32),
                vmem((ny - 1, fd, 128), F32),
                vmem((nz - 1, fd, 128), F32),
                vmem((ndp - 1, fd, 128), F32),
                vmem((nx, width, pr), BF16),
                vmem((nx, width, pr), BF16),
                vmem((nx - 1, width, pr), BF16),
                vmem((nx - 1, width, pr), BF16),
                sem, sem,
                sem((2, nz // 2)), sem((2, nz // 2)),
                sem, sem((nz - 1,)),
                sem, sem,
                sem, sem((nx - 1,)),
                sem, sem,
                sem((2, 2)), sem((2, 2)),
                sem((2, 2)), sem((2, 2)),
                sem((2, 2)), sem((2, 2)),
                sem((2,)), sem((2,)),
                sem((3,)), sem((3,)),
                sem, sem((nx,)),
                sem, sem,
            ],
            compiler_params=pltpu.CompilerParams(
                collective_id=0, has_side_effects=True, vmem_limit_bytes=56 * 2**20
            ),
        )(first, second, protos, pairing.reshape(fd, 128))
        return grad, loss[0, 0]

    return jax.shard_map(
        local,
        mesh=mesh,
        in_specs=(
            P(("dp", "proto"), None),
            P(("dp", "proto"), None),
            P(("dp", "proto"), None),
            P("dp"),
        ),
        out_specs=(P(("dp", "proto"), None), P()),
        check_vma=False,
    )
```

time: 702 us -> 123 us (0.18); the launches traced: 692 us -> 123 us
  blocking collectives: 430 us -> 0 us
  Pallas kernels: 0 us -> 118 us
  matrix products: 106 us -> 0 us
  waiting for transfers between devices: 99.4 us -> 0 us
  other arithmetic: 29.6 us -> 0 us
  between operations: 15.9 us -> 2.34 us
  local copies, waits for them, and re-layouts: 11.4 us -> 1.87 us
    psum x7 -> x0, blocking collectives: 430 us -> none  [the longest x3 231 us: row_pass(): return 1.0 / lax.psum(sample_slice, 'proto')]
    pallas_call x0 -> x1, Pallas kernels: none -> 118 us  [local(): pl.pallas_call(functools.partial(kernel, sizes), out_shape=(jax.ShapeDtyp...]
    dot_general x8 -> x0, matrix products: 106 us -> none  [the longest x3 57.3 us: normalize_cluster_axis(): jnp.einsum('wfy,wy->wf', optimal_transport_solver, cluster_factor, precis...]
    all_gather x2 -> x0, waiting for transfers between devices: 99.3 us -> none  [the longest x1 73.5 us: local(): gathered = lax.all_gather(stacked, 'proto', axis=1, tiled=True)]
    reduce_sum x4 -> x0, other arithmetic: 15.4 us -> none  [the longest x1 12.5 us: local(): jnp.sum(swapped * (log_total[:, :, None] - centroid_similarity / SOFT_TEMP))]
    mul x1 -> x0, other arithmetic: 7.35 us -> none  [local(): sample_factor[:, :, None] * optimal_transport_solver]
  transfers between devices with their start and end apart: 3 -> 0, of which waited for: 2 -> 0; matrix products, arithmetic and copies ran while one was open for 1% -> 0% of each run, Pallas kernels for 0% -> 0%
where the time goes in v1:
time: 123 us
  Pallas kernels  118 us (96%)
  between operations  2.34 us (2%)
  local copies, waits for them, and re-layouts  1.87 us (2%)
    pallas_call x1, Pallas kernels, local(): pl.pallas_call(functools.partial(kernel, sizes), out_shape=(jax.ShapeDtyp...  118 us

profile of v1, /device:TPU:1, one launch (start us, length us, event | category | flops | bytes accessed | tf_op | source)
XLA Modules:
  0.0 122.7 jit_solution(56821308649591216)
XLA Ops:
  0.6 118.4 %shard_map.59 = (f32[256,512]{1,0:T(8,128)}, f32[1,1]{1,0:T(1,128)}) custom-call(bf16[32,512]{1,0:T(8,128)(2,1)} %first_ref.1, bf16[32,512]{1,0:T(8,128)(2,1)} %second_ref.1, f32[256,512]{1,0:T(8,128)} %protos_ref.1, s32[8,128]{1,0:T(8,128)} %bitcast.2), custom_call_target="tpu_custom_call" | custom-call | tf_op jit(solution)/shard_map/pallas_call | solution.py:587
  119.1 1.9 %copy.8 = f32[256,512]{1,0:T(8,128)} copy(f32[256,512]{1,0:T(8,128)} %get-tuple-element.8) | data formatting | bytes 1048576

commit v2 on v1

--- a/solution.py
+++ b/solution.py
@@ -10,6 +10,7 @@
 
 ITERS = 3
 SOFT_TEMP = 0.1
+LOG2_E = math.log2(math.e)
 NORM_EPS = 1e-06
 CORES = 2
 DEPTH = 8
@@ -56,7 +57,7 @@
     p_ref,
     onehot_ref,
     ut_ref,
-    e_ref,
+    k_ref,
     acc_ref,
     soft_acc_ref,
     rb_ref,
@@ -148,6 +149,26 @@
     zs = [at(dz=d) for d in range(1, nz)]
     dps = [at(dx=d, dc=e) for d in range(nx) for e in range(CORES) if d or e]
 
+    half = ny // 2
+    last = nz // 2
+
+    def ring_ways(step, q):
+        return [way for way in range(2) if step < last or (q < half) == (way == 0)]
+
+    def ring_chunk(step, q, way):
+        far = nz - step if way == 0 else step
+        return v_ref.at[0, lax.rem(z + far, nz), lax.rem(y + ny - q, ny)]
+
+    def ring_send(step, q):
+        for way in ring_ways(step, q):
+            chunk = ring_chunk(step - 1, q, way)
+            to = zs[0] if way == 0 else zs[nz - 2]
+            send(chunk, chunk, az_s, az_r.at[way, step - 1, q], to)
+
+    def ring_wait(step, q):
+        for way in ring_ways(step, q):
+            drain(ring_chunk(step, q, way), az_r.at[way, step - 1, q])
+
     barrier = pltpu.get_barrier_semaphore()
     for device in dps + ys + zs:
         pl.semaphore_signal(
@@ -158,20 +179,16 @@
     p_ref[dp] = unit_rows(protos_ref[...])
     pl.semaphore_wait(barrier, len(dps) + len(ys) + len(zs))
 
-    for device in ys:
-        send(v_ref.at[0, z, y], v_ref.at[0, z, y], ay_s, ay_r, device)
+    for j, device in enumerate(ys):
+        send(v_ref.at[0, z, y], v_ref.at[0, z, y], ay_s, ay_r.at[j], device)
+    ring_send(1, 0)
     for j, device in enumerate(xs):
         send(p_ref.at[dp], p_ref.at[dp], px_s, px_r.at[j], device)
-    z_order = []
-    for d in range(1, nz // 2 + 1):
-        z_order.append(d)
-        if nz - d != d:
-            z_order.append(nz - d)
-    for d in z_order:
+    for d in sorted(range(1, nz), key=lambda d: min(d, nz - d)):
         send(v_ref.at[1, z, y], v_ref.at[1, z, y], bz_s, bz_r.at[d - 1], zs[d - 1])
-    send(p_ref.at[dp], p_ref.at[dp], ps_s, ps_r, sib)
     for device in ys:
         send(v_ref.at[1, z, y], v_ref.at[1, z, y], by_s, by_r, device)
+    send(p_ref.at[dp], p_ref.at[dp], ps_s, ps_r, sib)
 
     pair = pair_ref[...]
     where = (pair % (nz * fr) // fr) * group + (pair // (nz * fr)) * fr + pair % fr
@@ -196,73 +213,61 @@
         for device in ys:
             send(v_ref.at[1, zb, y], v_ref.at[1, zb, y], by_s, by_r, device)
 
-    half = ny // 2
-
-    def ring_blocks(step):
-        up = lax.rem(z + nz - (step - 1), nz)
-        down = lax.rem(z + step - 1, nz)
-        if step < nz // 2:
-            return v_ref.at[0, up], v_ref.at[0, down]
-        return v_ref.at[0, up, pl.ds(0, half)], v_ref.at[0, down, pl.ds(half, half)]
-
-    def ring_send(step):
-        up, down = ring_blocks(step)
-        send(up, up, az_s.at[0, step - 1], az_r.at[0, step - 1], zs[0])
-        send(down, down, az_s.at[1, step - 1], az_r.at[1, step - 1], zs[nz - 2])
-
-    def ring_wait(step):
-        up, down = ring_blocks(step)
-        drain(up, az_r.at[0, step - 1])
-        drain(down, az_r.at[1, step - 1])
-
     def wait_protos_x(j):
         owner = lax.rem(x + nx - (j + 1), nx) * CORES + core
         drain(p_ref.at[owner], px_r.at[j])
         send(p_ref.at[owner], p_ref.at[owner], ps_s, ps_r, sib)
 
-    def first_pass(view, rows, row, block):
+    def first_pass(view, starts, block):
         count = block.shape[0]
-
-        def step(j, carry):
-            cols = pl.ds(pl.multiple_of(j * pr, pr), pr)
+        each = count // len(starts)
+        soft = jnp.zeros((count, 128), F32)
+        for j in range(nx * CORES):
             scores = lax.dot_general(block, p_ref[j], NT, preferred_element_type=F32)
-            e = jnp.exp(scores / SOFT_TEMP)
-            e_ref[view, rows, cols] = e
-            total = e[:, 0:128]
-            for t in range(1, tiles_pr):
-                total = total + e[:, t * 128 : (t + 1) * 128]
-            soft_acc_ref[view, rows, :] += total
-            cs_ref[view, :, cols] += jnp.sum((e * e).reshape(count // 8, 8, pr), axis=0)
-            return carry
-
-        lax.fori_loop(0, nx * CORES, step, 0)
-
-    def zero_block(zb):
-        rows = pl.ds(pl.multiple_of(zb * group, group), group)
-        first_pass(0, rows, zb, v_ref[0, zb].reshape(group, width))
-
-    drain(v_ref.at[0, 0, pl.ds(0, ny - 1)], ay_r)
-    ring_send(1)
-    near = z_order[: (nz - 1) // 2]
-    far = z_order[(nz - 1) // 2 :]
-    for d in near:
-        wait_frames_z(d)
-    if nz // 2 > 1:
-        ring_wait(1)
-        ring_send(2)
-    for d in far:
-        wait_frames_z(d)
-    x_order = sorted(range(nx - 1), key=lambda j: min(j + 1, nx - j - 1))
-    for j in x_order[:-1]:
-        wait_protos_x(j)
-    for step in range(3, nz // 2):
-        ring_wait(step - 1)
-        ring_send(step)
-    wait_protos_x(x_order[-1])
+            e = jnp.exp2(scores * (LOG2_E / SOFT_TEMP))
+            k = e * e
+            for i, start in enumerate(starts):
+                rows = pl.ds(pl.multiple_of(start, each), each)
+                k_ref[view, rows, j * pr : (j + 1) * pr] = k[i * each : (i + 1) * each]
+            for t in range(tiles_pr):
+                soft = soft + e[:, t * 128 : (t + 1) * 128]
+            cs_ref[view, :, j * pr : (j + 1) * pr] += jnp.sum(
+                k.reshape(count // 8, 8, pr), axis=0
+            )
+        for i, start in enumerate(starts):
+            rows = pl.ds(pl.multiple_of(start, each), each)
+            soft_acc_ref[view, rows, :] = soft[i * each : (i + 1) * each]
+
+    def zero_pair(one, two):
+        block = jnp.concatenate(
+            [v_ref[0, one].reshape(group, width), v_ref[0, two].reshape(group, width)], axis=0
+        )
+        first_pass(0, [one * group, two * group], block)
+
+    def frames_y(j):
+        drain(v_ref.at[0, z, lax.rem(y + ny - (j + 1), ny)], ay_r.at[j])
+        ring_send(1, j + 1)
+
+    def ring_next(step, q):
+        ring_wait(step, q)
+        ring_send(step + 1, q)
+
+    events = []
+    for j in range(ny - 1):
+        events.append((3.6 + 0.3 * j, functools.partial(frames_y, j)))
+    for step in range(1, last):
+        for q in range(ny):
+            when = (4.5 if q else 0.0) + 3.3 * step + 0.65 * q
+            events.append((when, functools.partial(ring_next, step, q)))
+    for d in range(1, nz):
+        when = 3.0 + 1.7 * min(d, nz - d) + 0.01 * d
+        events.append((when, functools.partial(wait_frames_z, d)))
+    for j in range(nx - 1):
+        when = 6.0 + 3.5 * min(j + 1, nx - j - 1) + 0.01 * j
+        events.append((when, functools.partial(wait_protos_x, j)))
+    for when, event in sorted(events, key=lambda pair: pair[0]):
+        event()
     drain(p_ref.at[pl.ds(0, nx)], ps_r)
-    if nz // 2 > 2:
-        ring_wait(nz // 2 - 1)
-        ring_send(nz // 2)
     drain(v_ref.at[1, :, pl.ds(0, ny - 1)], by_r)
 
     chunk = min(256, frames)
@@ -275,7 +280,7 @@
             NN,
             preferred_element_type=F32,
         ).astype(BF16)
-        first_pass(1, rows, i, partner_ref[rows, :])
+        first_pass(1, [i * chunk], partner_ref[rows, :])
         return carry
 
     lax.fori_loop(0, frames // chunk, permute, 0)
@@ -354,8 +359,8 @@
             rows = pl.ds(pl.multiple_of(i * 64, 64), 64)
             total = jnp.zeros((64, 128), F32)
             for t in range(ptiles):
-                e = e_ref[view, rows, t * 128 : (t + 1) * 128]
-                total = total + (e * e) * c_ref[view, t : t + 1, :]
+                k = k_ref[view, rows, t * 128 : (t + 1) * 128]
+                total = total + k * c_ref[view, t : t + 1, :]
             acc_ref[view, rows, :] = total
             return carry
 
@@ -368,10 +373,8 @@
             scale = rb_ref[view, rows, :]
             out = []
             for t in range(ptiles):
-                e = e_ref[view, rows, t * 128 : (t + 1) * 128]
-                out.append(
-                    totals[t] + jnp.sum(((e * e) * scale).reshape(4, 8, 128), axis=0)
-                )
+                k = k_ref[view, rows, t * 128 : (t + 1) * 128]
+                out.append(totals[t] + jnp.sum((k * scale).reshape(4, 8, 128), axis=0))
             return tuple(out)
 
         totals = lax.fori_loop(
@@ -381,12 +384,15 @@
             cs_ref[view, :, t * 128 : (t + 1) * 128] = totals[t]
 
     dp_start(1, 0, column_totals(1))
-    for d in range(nz // 2):
-        zero_block(lax.rem(z + d, nz))
-        if d:
-            zero_block(lax.rem(z + nz - d, nz))
-    ring_wait(nz // 2)
-    zero_block(lax.rem(z + nz // 2, nz))
+
+    def pairs(i, carry):
+        zero_pair(lax.rem(z + i, nz), lax.rem(z + nz - i, nz))
+        return carry
+
+    lax.fori_loop(1, last, pairs, 0)
+    for q in range(ny):
+        ring_wait(last, q)
+    zero_pair(z, lax.rem(z + last, nz))
     dp_start(0, 0, column_totals(0))
 
     for view in range(2):
@@ -446,12 +452,12 @@
                 rows = pl.ds(pl.multiple_of(i * 32, 32), 32)
                 sums = [jnp.zeros((32, 128), F32), jnp.zeros((32, 128), F32)]
                 for t in range(ptiles):
-                    e = [e_ref[v, rows, t * 128 : (t + 1) * 128] for v in range(2)]
+                    k = [k_ref[v, rows, t * 128 : (t + 1) * 128] for v in range(2)]
                     for v in range(2):
-                        term = (e[v] * e[v]) * c_ref[v, t : t + 1, :]
-                        sums[v] = sums[v] + term * jnp.log(e[1 - v])
+                        term = k[v] * c_ref[v, t : t + 1, :]
+                        sums[v] = sums[v] + term * jnp.log(k[1 - v])
                 for v in range(2):
-                    acc_ref[v, rows, :] = sums[v]
+                    acc_ref[v, rows, :] = 0.5 * sums[v]
                 return carry
 
             lax.fori_loop(0, frames // 32, step, 0)
@@ -498,14 +504,14 @@
             for t in range(tiles_pr):
                 tile = owner * tiles_pr + t
                 cols = pl.ds(pl.multiple_of(tile * 128, 128), 128)
-                e = [e_ref[v, rows, cols] for v in range(2)]
+                k = [k_ref[v, rows, cols] for v in range(2)]
                 assigned = [
-                    (e[v] * e[v]) * (rb_ref[v, rows, :] * c_ref[v, pl.ds(tile, 1), :])
+                    k[v] * (rb_ref[v, rows, :] * c_ref[v, pl.ds(tile, 1), :])
                     for v in range(2)
                 ]
                 for v in range(2):
                     w_ref[v, rows, t * 128 : (t + 1) * 128] = (
-                        e[v] * sb_ref[v, rows, :] - assigned[1 - v]
+                        (k[v] * lax.rsqrt(k[v])) * sb_ref[v, rows, :] - assigned[1 - v]
                     ).astype(BF16)
             return carry
 
@@ -547,10 +553,7 @@
     loss_ref[0, 0] = jnp.sum(total) / (2.0 * frames * nx * CORES)
 
     drain(v_ref.at[0, 0, pl.ds(0, ny - 1)], ay_s)
-    for step in range(1, nz // 2 + 1):
-        up, down = ring_blocks(step)
-        drain(up, az_s.at[0, step - 1])
-        drain(down, az_s.at[1, step - 1])
+    drain(v_ref.at[0, pl.ds(0, nz - 1)], az_s)
     drain(v_ref.at[1, pl.ds(0, nz - 1), 0], bz_s)
     drain(v_ref.at[1, :, pl.ds(0, ny - 1)], by_s)
     drain(p_ref.at[pl.ds(0, nx - 1)], px_s)
@@ -631,8 +634,8 @@
                 vmem((nx, width, pr), BF16),
                 vmem((nx - 1, width, pr), BF16),
                 vmem((nx - 1, width, pr), BF16),
-                sem, sem,
-                sem((2, nz // 2)), sem((2, nz // 2)),
+                sem, sem((ny - 1,)),
+                sem, sem((2, nz // 2, ny)),
                 sem, sem((nz - 1,)),
                 sem, sem,
                 sem, sem((nx - 1,)),

time: 123 us -> 103 us (0.84)
  Pallas kernels: 118 us -> 98.9 us
    pallas_call x1, Pallas kernels: 118 us -> 98.9 us  [local(): pl.pallas_call(functools.partial(kernel, sizes), out_shape=(jax.ShapeDtyp...]
where the time goes in v2:
time: 103 us
  Pallas kernels  98.9 us (96%)
  between operations  2.34 us (2%)
  local copies, waits for them, and re-layouts  1.87 us (2%)
    pallas_call x1, Pallas kernels, local(): pl.pallas_call(functools.partial(kernel, sizes), out_shape=(jax.ShapeDtyp...  98.9 us

profile of v2, /device:TPU:1, one launch (start us, length us, event | category | flops | bytes accessed | tf_op | source)
XLA Modules:
  0.0 103.1 jit_solution(12541502960491221956)
XLA Ops:
  0.6 98.9 %shard_map.59 = (f32[256,512]{1,0:T(8,128)}, f32[1,1]{1,0:T(1,128)}) custom-call(bf16[32,512]{1,0:T(8,128)(2,1)} %first_ref.1, bf16[32,512]{1,0:T(8,128)(2,1)} %second_ref.1, f32[256,512]{1,0:T(8,128)} %protos_ref.1, s32[8,128]{1,0:T(8,128)} %bitcast.2), custom_call_target="tpu_custom_call" | custom-call | tf_op jit(solution)/shard_map/pallas_call | solution.py:590
  99.5 1.9 %copy.8 = f32[256,512]{1,0:T(8,128)} copy(f32[256,512]{1,0:T(8,128)} %get-tuple-element.8) | data formatting | bytes 1048576

commit v3 on v2

v3 whole, which is shorter than its diff:
```python
import functools
import math

import jax
import jax.numpy as jnp
from jax import lax
from jax.experimental import pallas as pl
from jax.experimental.pallas import tpu as pltpu
from jax.sharding import PartitionSpec as P

ITERS = 3
SOFT_TEMP = 0.1
LOG2_E = math.log2(math.e)
NORM_EPS = 1e-06
CORES = 2
DEPTH = 8

F32 = jnp.float32
BF16 = jnp.bfloat16
NT = (((1,), (1,)), ((), ()))
NN = (((1,), (0,)), ((), ()))


def unit_rows(matrix):
    widened = matrix.astype(F32)
    return (
        widened * lax.rsqrt(jnp.sum(widened * widened, axis=-1, keepdims=True) + NORM_EPS)
    ).astype(BF16)


def drain(ref, sem):
    pltpu.make_async_copy(ref, ref, sem).wait()


def rows_to_lanes(acc_ref, view, out_ref, rows):
    for b in range(rows // 128):
        block = acc_ref[view, b * 128 : (b + 1) * 128, :]
        out_ref[b : b + 1, :] = jnp.sum(block.T, axis=0, keepdims=True)


def lanes_to_rows(dense, out_ref, view, rows):
    for b in range(rows // 128):
        block = jnp.broadcast_to(dense[b : b + 1, :], (128, 128))
        out_ref[view, b * 128 : (b + 1) * 128, :] = block.T


def kernel(
    sizes,
    first_ref,
    second_ref,
    protos_ref,
    pair_ref,
    grad_ref,
    loss_ref,
    v_ref,
    partner_ref,
    p_ref,
    onehot_ref,
    ut_ref,
    k_ref,
    ka_ref,
    acc_ref,
    soft_acc_ref,
    rb_ref,
    sb_ref,
    cs_ref,
    c_ref,
    r_ref,
    row_ref,
    t_ref,
    w_ref,
    g_ref,
    dp_src,
    dp_buf,
    y_src,
    y_buf,
    z_src,
    z_buf,
    soft_src,
    soft_ybuf,
    soft_mid,
    soft_zbuf,
    loss_src,
    loss_ybuf,
    loss_zbuf,
    loss_xbuf,
    ss_ref,
    sr_ref,
    xs_ref,
    xr_ref,
    xo_ref,
    ay_s,
    ay_r,
    zr_s,
    zr_r,
    zo_s,
    zo_r,
    fy_s,
    fy_r,
    px_s,
    px_r,
    po_r,
    ps_s,
    ps_r,
    dp_s,
    dp_r,
    y_s,
    y_r,
    z_s,
    z_r,
    soft_s,
    soft_r,
    loss_s,
    loss_r,
    ss_s,
    ss_r,
    xs_s,
    xs_r,
    xo_s,
    xo_r,
):
    nx, ny, nz, fr, width, pr = sizes
    frames = fr * ny * nz
    group = fr * ny
    protos = pr * nx * CORES
    ptiles = protos // 128
    tiles_pr = pr // 128
    fdense = frames // 128
    grad_scale = protos * ny * nz / (SOFT_TEMP * math.sqrt(2.0 * frames * nx * CORES))

    dp, pi = lax.axis_index("dp"), lax.axis_index("proto")
    x, core = dp // CORES, dp % CORES
    y, z = pi // nz, pi % nz

    def at(dx=0, dc=0, dy=0, dz=0):
        return {
            "dp": lax.rem(x + dx, nx) * CORES + lax.rem(core + dc, CORES),
            "proto": lax.rem(y + dy, ny) * nz + lax.rem(z + dz, nz),
        }

    def send(src, dst, ssem, rsem, device):
        pltpu.make_async_remote_copy(
            src_ref=src,
            dst_ref=dst,
            send_sem=ssem,
            recv_sem=rsem,
            device_id=device,
            device_id_type=pl.DeviceIdType.MESH,
        ).start()

    sib = at(dc=1)
    xs = [at(dx=d) for d in range(1, nx)]
    ys = [at(dy=d) for d in range(1, ny)]
    zs = [at(dz=d) for d in range(1, nz)]
    dps = [at(dx=d, dc=e) for d in range(nx) for e in range(CORES) if d or e]

    last = nz // 2
    near = max(1, last - 2)
    split = near > 1

    def chunk(dz, q=0):
        return v_ref.at[lax.rem(z + nz + dz, nz), lax.rem(y + ny - q, ny)]

    def ring_send(step, q):
        for way, sign in enumerate((-1, 1)):
            part = chunk(sign * (step - 1), q)
            if q and split and step == near:
                part = part.at[0]
            send(part, part, zr_s.at[min(q, 1)], zr_r.at[way, step - 1, q], zs[0 if way == 0 else nz - 2])

    def ring_skip():
        for way in range(2):
            to = zs[1 if way == 0 else nz - 3]
            send(chunk(0), chunk(0), zr_s.at[0], zr_r.at[way, 1, 0], to)

    def ring_wait(step, q):
        for way, sign in enumerate((-1, 1)):
            part = chunk(sign * step, q)
            drain(part.at[0] if q and split and step == near else part, zr_r.at[way, step - 1, q])

    def far_part(dz):
        return chunk(dz).at[1] if abs(dz) == near else chunk(dz)

    def far_send(dz, index):
        for device in ys:
            send(far_part(dz), far_part(dz), fy_s, fy_r.at[index], device)

    def far_wait(dz, index):
        block = v_ref.at[lax.rem(z + nz + dz, nz), pl.ds(0, ny - 1)]
        drain(block.at[:, 1] if abs(dz) == near else block, fy_r.at[index])

    def far_index(dz):
        if dz == last:
            return 0
        return 2 * (abs(dz) - near) + (1 if dz < 0 else 2)

    half = pr // 2

    def proto_half(dx, part):
        owner = lax.rem(x + nx + dx, nx) * CORES + core
        return p_ref.at[owner, pl.ds(part * half, half)]

    def proto_near(way, part):
        piece = proto_half(-1 if way == 0 else 1, part)
        drain(piece, px_r.at[way, part])
        if part == way:
            send(piece, piece, px_s, po_r.at[part], xs[0 if way == 0 else nx - 2])
        send(piece, piece, ps_s, ps_r, sib)

    def proto_far(part):
        piece = proto_half(2, part)
        drain(piece, po_r.at[part])
        send(piece, piece, ps_s, ps_r, sib)

    barrier = pltpu.get_barrier_semaphore()
    for device in dps + ys + zs:
        pl.semaphore_signal(
            barrier, inc=1, device_id=device, device_id_type=pl.DeviceIdType.MESH
        )
    v_ref[z, y, 0] = unit_rows(first_ref[...])
    v_ref[z, y, 1] = unit_rows(second_ref[...])
    p_ref[dp] = unit_rows(protos_ref[...])
    pl.semaphore_wait(barrier, len(dps) + len(ys) + len(zs))

    for j, device in enumerate(ys):
        send(chunk(0), chunk(0), ay_s, ay_r.at[j], device)
    if last > 2:
        ring_skip()
    send(chunk(0), chunk(0), zo_s, zo_r, zs[last - 1])
    ring_send(1, 0)
    for part in range(2):
        for way in range(2):
            piece = proto_half(0, part if way == 0 else 1 - part)
            where = px_r.at[way, part if way == 0 else 1 - part]
            send(piece, piece, px_s, where, xs[0 if way == 0 else nx - 2])
    send(p_ref.at[dp], p_ref.at[dp], ps_s, ps_r, sib)

    pair = pair_ref[...]
    where = (pair % (nz * fr) // fr) * group + (pair // (nz * fr)) * fr + pair % fr
    where = where.astype(F32)
    for b in range(fdense):
        column = jnp.broadcast_to(where[b : b + 1, :], (128, 128)).T
        for t in range(fdense):
            lane = (lax.broadcasted_iota(jnp.int32, (128, 128), 1) + t * 128).astype(F32)
            block = jnp.where(column == lane, 1.0, 0.0).astype(BF16)
            for q in range(128 // fr):
                natural = b * 128 + q * fr
                row = (natural % (nz * fr) // fr) * group + natural // (nz * fr) * fr
                onehot_ref[row : row + fr, t * 128 : (t + 1) * 128] = block[
                    q * fr : (q + 1) * fr, :
                ]
    cs_ref[...] = jnp.zeros_like(cs_ref)
    soft_acc_ref[...] = jnp.zeros_like(soft_acc_ref)

    def first_pass(view, starts, block):
        count = block.shape[0]
        each = count // len(starts)
        soft = jnp.zeros((count, 128), F32)
        for j in range(nx * CORES):
            scores = lax.dot_general(block, p_ref[j], NT, preferred_element_type=F32)
            e = jnp.exp2(scores * (LOG2_E / SOFT_TEMP))
            k = e * e
            for i, start in enumerate(starts):
                rows = pl.ds(pl.multiple_of(start, each), each)
                k_ref[view, rows, j * pr : (j + 1) * pr] = k[i * each : (i + 1) * each]
            for t in range(tiles_pr):
                soft = soft + e[:, t * 128 : (t + 1) * 128]
            cs_ref[view, :, j * pr : (j + 1) * pr] += jnp.sum(
                k.reshape(count // 8, 8, pr), axis=0
            )
        for i, start in enumerate(starts):
            rows = pl.ds(pl.multiple_of(start, each), each)
            soft_acc_ref[view, rows, :] = soft[i * each : (i + 1) * each]

    def frames_y(q):
        drain(chunk(0, q), ay_r.at[q - 1])
        ring_send(1, q)

    def ring_next(step, q):
        ring_wait(step, q)
        if (1 < step < last - 1) if q == 0 else step < near:
            ring_send(step + 1, q)
        if q == 0 and (step > near or (split and step == near)):
            far_send(-step, far_index(-step))
            far_send(step, far_index(step))

    def opposite():
        drain(chunk(last), zo_r)
        far_send(last, far_index(last))

    events = [(6.5, opposite)]
    for q in range(1, ny):
        events.append((4.0 + 0.5 * q, functools.partial(frames_y, q)))
    for step in range(1, last):
        when = 7.0 if step == 1 else 3.9 + 5.0 * (step - 2)
        events.append((when, functools.partial(ring_next, step, 0)))
    for q in range(1, ny):
        for step in range(1, near):
            when = 6.0 + 3.5 * step + 1.3 * q
            events.append((when, functools.partial(ring_next, step, q)))
    for way in range(2):
        events.append((6.0 + 0.1 * way, functools.partial(proto_near, way, way)))
        events.append((8.6 + 0.1 * way, functools.partial(proto_near, way, 1 - way)))
        events.append((12.0 + 0.1 * way, functools.partial(proto_far, way)))
    for when, event in sorted(events, key=lambda pair: pair[0]):
        event()
    drain(p_ref.at[pl.ds(0, nx)], ps_r)

    def pair_wait(p):
        if p == 0:
            if near == 1:
                for q in range(1, ny):
                    ring_wait(1, q)
        elif p == 1:
            far_wait(last, far_index(last))
        else:
            step = last + 1 - p
            if step <= near:
                for q in range(1, ny):
                    ring_wait(step, q)
            far_wait(-step, far_index(-step))
            far_wait(step, far_index(step))

    def pair_pass(n, carry):
        p, view = n // 2, n % 2
        for known in range(last):

            @pl.when(n == 2 * known)
            def _(known=known):
                pair_wait(known)

        step = lax.max(1, (last + 1 - p) * lax.min(p, 1))
        one = lax.rem(z + step, nz)
        two = lax.rem(z + nz - step * lax.min((p - 1) * (p - 1), 1), nz)
        block = jnp.concatenate(
            [v_ref[b, :, view].reshape(group, width) for b in (one, two)], axis=0
        )
        first_pass(view, [one * group, two * group], block)
        return carry

    lax.fori_loop(0, 2 * last, pair_pass, 0)

    def dp_start(view, it, source):
        slot = it % 2

        @pl.when(it >= 2)
        def _():
            drain(dp_buf.at[view, slot], dp_s.at[view, slot])

        dp_src[view, slot] = source
        for j, device in enumerate(dps):
            send(
                dp_src.at[view, slot],
                dp_buf.at[view, slot, j],
                dp_s.at[view, slot],
                dp_r.at[view, slot],
                device,
            )

    def dp_wait(view, it):
        slot = it % 2
        drain(dp_buf.at[view, slot], dp_r.at[view, slot])
        total = dp_src[view, slot]
        for j in range(len(dps)):
            total = total + dp_buf[view, slot, j]
        return total

    def y_start(view, it):
        slot = it % 2

        @pl.when(it >= 2)
        def _():
            drain(y_buf.at[view, slot], y_s.at[view, slot])

        y_src[view, slot] = row_ref[view]
        for j, device in enumerate(ys):
            send(
                y_src.at[view, slot],
                y_buf.at[view, slot, j],
                y_s.at[view, slot],
                y_r.at[view, slot],
                device,
            )

    def y_wait(view, it):
        slot = it % 2
        drain(y_buf.at[view, slot], y_r.at[view, slot])
        total = y_src[view, slot]
        for j in range(len(ys)):
            total = total + y_buf[view, slot, j]

        @pl.when(it >= 2)
        def _():
            drain(z_buf.at[view, slot], z_s.at[view, slot])

        z_src[view, slot] = total
        for j, device in enumerate(zs):
            send(
                z_src.at[view, slot],
                z_buf.at[view, slot, j],
                z_s.at[view, slot],
                z_r.at[view, slot],
                device,
            )

    def z_wait(view, it):
        slot = it % 2
        drain(z_buf.at[view, slot], z_r.at[view, slot])
        total = z_src[view, slot]
        for j in range(len(zs)):
            total = total + z_buf[view, slot, j]
        return total

    def column_totals(view):
        parts = [
            jnp.sum(cs_ref[view, :, t * 128 : (t + 1) * 128], axis=0, keepdims=True)
            for t in range(ptiles)
        ]
        return jnp.concatenate(parts, axis=0)

    def frame_sums(view):
        def step(b, carry):
            rows = pl.ds(pl.multiple_of(b * 128, 128), 128)
            total = jnp.zeros((128, 128), F32)
            for t in range(ptiles):
                k = k_ref[view, rows, t * 128 : (t + 1) * 128]
                total = total + k * c_ref[view, t : t + 1, :]
            row_ref[view, pl.ds(b, 1), :] = jnp.sum(total.T, axis=0, keepdims=True)
            return carry

        lax.fori_loop(0, fdense, step, 0, unroll=min(4, fdense))

    def proto_sums(view):
        def step(i, totals):
            rows = pl.ds(pl.multiple_of(i * 64, 64), 64)
            scale = rb_ref[view, rows, :]
            out = []
            for t in range(ptiles):
                k = k_ref[view, rows, t * 128 : (t + 1) * 128]
                out.append(totals[t] + jnp.sum((k * scale).reshape(8, 8, 128), axis=0))
            return tuple(out)

        totals = lax.fori_loop(
            0,
            frames // 64,
            step,
            tuple(jnp.zeros((8, 128), F32) for _ in range(ptiles)),
            unroll=2,
        )
        for t in range(ptiles):
            cs_ref[view, :, t * 128 : (t + 1) * 128] = totals[t]

    zero = jnp.int32(0)
    dp_start(1, zero, column_totals(1))
    dp_start(0, zero, column_totals(0))

    for view in range(2):
        rows_to_lanes(soft_acc_ref, view, soft_src.at[pl.ds(view * fdense, fdense)], frames)
    for j, device in enumerate(ys):
        send(soft_src, soft_ybuf.at[j], soft_s.at[0], soft_r.at[0], device)

    eye = jnp.where(
        lax.broadcasted_iota(jnp.int32, (width, width), 0)
        == lax.broadcasted_iota(jnp.int32, (width, width), 1),
        1.0,
        0.0,
    ).astype(BF16)

    rows_each = min(256, frames)
    pieces = frames // rows_each

    def transpose_view(view):
        for i in range(pieces):
            if view:
                block = partner_ref[i * rows_each : (i + 1) * rows_each, :]
            else:
                count = rows_each // group
                block = v_ref[i * count : (i + 1) * count, :, 0].reshape(rows_each, width)
            ut_ref[view, :, i * rows_each : (i + 1) * rows_each] = lax.dot_general(
                eye, block, NT, preferred_element_type=F32
            ).astype(BF16)

    def align_rows():
        second = v_ref[:, :, 1].reshape(frames, width)
        for i in range(pieces):
            rows = slice(i * rows_each, (i + 1) * rows_each)
            partner_ref[rows, :] = lax.dot_general(
                onehot_ref[rows, :], second, NN, preferred_element_type=F32
            ).astype(BF16)

    def align_kernel(first, count):
        def step(i, carry):
            rows = pl.ds(pl.multiple_of(i * rows_each, rows_each), rows_each)
            block = partner_ref[rows, :]
            for j in range(nx * CORES):
                scores = lax.dot_general(block, p_ref[j], NT, preferred_element_type=F32)
                ka_ref[rows, j * pr : (j + 1) * pr] = jnp.exp2(
                    scores * (2.0 * LOG2_E / SOFT_TEMP)
                )
            return carry

        lax.fori_loop(first, first + count, step, 0)

    def align_dense(dense):
        row = jnp.concatenate([dense[b : b + 1, :] for b in range(fdense)], axis=1)
        high = row.astype(BF16).astype(F32)
        middle = (row - high).astype(BF16).astype(F32)
        low = row - high - middle
        parts = jnp.concatenate([high, middle, low, jnp.zeros((13, frames), F32)], axis=0)
        out = lax.dot_general(
            parts.astype(BF16), onehot_ref[...], NT, preferred_element_type=F32
        )
        total = out[0:1] + out[1:2] + out[2:3]
        return jnp.concatenate(
            [total[:, b * 128 : (b + 1) * 128] for b in range(fdense)], axis=0
        )

    transpose_view(0)
    align_rows()

    def soft_rows():
        total = soft_src[...]
        drain(soft_ybuf, soft_r.at[0])
        for j in range(len(ys)):
            total = total + soft_ybuf[j]
        soft_mid[...] = total

    def soft_totals():
        drain(soft_zbuf, soft_r.at[1])
        total = soft_mid[...]
        for j in range(len(zs)):
            total = total + soft_zbuf[j]
        transpose_view(1)
        for view in range(2):
            dense = total[view * fdense : (view + 1) * fdense]
            if view:
                dense = align_dense(dense)
            lanes_to_rows(grad_scale / dense, sb_ref, view, frames)
            r_ref[2 + view] = jnp.log(dense)

    def cross_sums():
        def step(i, carry):
            rows = pl.ds(pl.multiple_of(i * 32, 32), 32)
            sums = [jnp.zeros((32, 128), F32) for _ in range(3)]
            for t in range(ptiles):
                k = [ref[rows, t * 128 : (t + 1) * 128] for ref in (k_ref.at[0], ka_ref)]
                terms = [k[v] * c_ref[v, t : t + 1, :] for v in range(2)]
                sums[0] = sums[0] + terms[0] * jnp.log(k[1])
                sums[1] = sums[1] + terms[1] * jnp.log(k[0])
                sums[2] = sums[2] + terms[1]
            acc_ref[0, rows, :] = 0.5 * sums[0]
            acc_ref[1, rows, :] = 0.5 * sums[1]
            soft_acc_ref[1, rows, :] = sums[2]
            return carry

        lax.fori_loop(0, frames // 32, step, 0)
        for v in range(2):
            rows_to_lanes(acc_ref, v, t_ref.at[v], frames)
        rows_to_lanes(soft_acc_ref, 1, row_ref.at[1], frames)

    def sweep(it, carry):
        for view in (1, 0):
            c_ref[view] = 1.0 / dp_wait(view, it)
            frame_sums(view)
            y_start(view, it)

        @pl.when(it == 0)
        def _():
            align_kernel(0, pieces // 2)
            soft_rows()

        for view in (1, 0):
            y_wait(view, it)

        @pl.when(it == 0)
        def _():
            for j, device in enumerate(zs):
                send(soft_mid, soft_zbuf.at[j], soft_s.at[1], soft_r.at[1], device)
            align_kernel(pieces // 2, pieces - pieces // 2)

        @pl.when(it == 1)
        def _():
            soft_totals()

        @pl.when(it == ITERS - 1)
        def _():
            cross_sums()

        for view in (1, 0):
            r_ref[view] = 1.0 / z_wait(view, it)

            @pl.when(it < ITERS - 1)
            def _(view=view):
                lanes_to_rows(r_ref[view], rb_ref, view, frames)
                proto_sums(view)
                dp_start(view, it + 1, column_totals(view))

            @pl.when(it == ITERS - 1)
            def _(view=view):
                if view:
                    r_ref[view] = align_dense(r_ref[view])
                lanes_to_rows(r_ref[view] * grad_scale, rb_ref, view, frames)

        return carry

    lax.fori_loop(0, ITERS, sweep, 0)

    loss = jnp.zeros((fdense, 128), F32)
    for v in range(2):
        loss = loss + r_ref[v] * (r_ref[3 - v] * row_ref[v] - t_ref[v])
    loss_src[0] = loss
    for j, device in enumerate(ys):
        send(loss_src.at[0], loss_ybuf.at[j], loss_s.at[0], loss_r.at[0], device)

    def loss_step(stage, buf, nextbuf, partners):
        drain(buf, loss_r.at[stage])
        total = loss_src[stage]
        for j in range(buf.shape[0]):
            total = total + buf[j]
        if nextbuf is None:
            return total
        loss_src[stage + 1] = total
        for j, device in enumerate(partners):
            send(
                loss_src.at[stage + 1],
                nextbuf.at[j],
                loss_s.at[stage + 1],
                loss_r.at[stage + 1],
                device,
            )
        return total

    def block_grad(owner):
        count = min(64, frames)
        for start in range(0, frames, count):
            rows = slice(start, start + count)
            for t in range(tiles_pr):
                tile = owner * tiles_pr + t
                cols = pl.ds(pl.multiple_of(tile * 128, 128), 128)
                k = [ref[rows, cols] for ref in (k_ref.at[0], ka_ref)]
                assigned = [
                    k[v] * (rb_ref[v, rows, :] * c_ref[v, pl.ds(tile, 1), :])
                    for v in range(2)
                ]
                for v in range(2):
                    w_ref[v, rows, t * 128 : (t + 1) * 128] = (
                        (k[v] * lax.rsqrt(k[v])) * sb_ref[v, rows, :] - assigned[1 - v]
                    ).astype(BF16)
        total = lax.dot_general(ut_ref[0], w_ref[0], NN, preferred_element_type=F32)
        total = total + lax.dot_general(ut_ref[1], w_ref[1], NN, preferred_element_type=F32)
        return total

    middle = width // 2
    lower, upper = pl.ds(0, middle), pl.ds(middle, middle)
    right, left = xs[0], xs[nx - 2]
    def scatter(n, carry):
        k, own = n // 2, n % 2
        d = (2 + 3 * k + (k // 2) * (3 - 2 * (k % 2))) % 4
        g_ref[k] = block_grad(lax.rem(x + d, nx) * CORES + lax.rem(core + 1 + own, CORES))

        @pl.when(own == 0)
        def _():
            ss_ref[k] = g_ref[k].astype(BF16)
            send(ss_ref.at[k], sr_ref.at[k], ss_s, ss_r.at[k], sib)

        @pl.when(own == 1)
        def _():
            drain(sr_ref.at[k], ss_r.at[k])

        @pl.when(n == 1)
        def _():
            xs_ref[0] = (g_ref[0] + sr_ref[0].astype(F32)).astype(BF16)
            send(xs_ref.at[0, lower], xo_ref.at[0], xo_s, xo_r.at[0], right)
            send(xs_ref.at[0, upper], xo_ref.at[1], xo_s, xo_r.at[1], left)

        @pl.when(n == 3)
        def _():
            xs_ref[1, upper] = (g_ref[1, upper] + sr_ref[1, upper].astype(F32)).astype(BF16)
            send(xs_ref.at[1, upper], xr_ref.at[0, upper], xs_s, xs_r, right)
            loss_step(0, loss_ybuf, loss_zbuf, zs)

        @pl.when(n == 5)
        def _():
            xs_ref[2, lower] = (g_ref[2, lower] + sr_ref[2, lower].astype(F32)).astype(BF16)
            send(xs_ref.at[2, lower], xr_ref.at[1, lower], xs_s, xs_r, left)
            for way, (rows, to) in enumerate(((lower, right), (upper, left))):
                drain(xo_ref.at[way], xo_r.at[way])
                xs_ref[1 + way, rows] = (
                    g_ref[1 + way, rows]
                    + sr_ref[1 + way, rows].astype(F32)
                    + xo_ref[way].astype(F32)
                ).astype(BF16)
                send(xs_ref.at[1 + way, rows], xr_ref.at[way, rows], xs_s, xs_r, to)

        return carry

    lax.fori_loop(0, 2 * nx, scatter, 0)
    loss_step(1, loss_zbuf, loss_xbuf, dps)
    drain(xr_ref, xs_r)
    for i in range(width // 128):
        for t in range(tiles_pr):
            rows, cols = slice(i * 128, (i + 1) * 128), slice(t * 128, (t + 1) * 128)
            total = g_ref[3, rows, cols] + sr_ref[3, rows, cols].astype(F32)
            for j in range(2):
                total = total + xr_ref[j, rows, cols].astype(F32)
            grad_ref[cols, rows] = total.T
    total = loss_step(2, loss_xbuf, None, None)
    loss_ref[0, 0] = jnp.sum(total) / (2.0 * frames * nx * CORES)

    drain(v_ref.at[0, pl.ds(0, ny - 1)], ay_s)
    drain(v_ref.at[pl.ds(0, 2 * (last - 1)), 0], zr_s.at[0])
    drain(v_ref.at[pl.ds(0, 2 * near - split), pl.ds(0, ny - 1)], zr_s.at[1])
    drain(chunk(0), zo_s)
    drain(v_ref.at[pl.ds(0, 2 * (last - 1 - near) + 1 + split), pl.ds(0, ny - 1)], fy_s)
    drain(p_ref.at[pl.ds(0, 3)], px_s)
    drain(p_ref.at[pl.ds(0, nx)], ps_s)
    for view in range(2):
        for slot in range(min(2, ITERS)):
            drain(dp_buf.at[view, slot], dp_s.at[view, slot])
            drain(y_buf.at[view, slot], y_s.at[view, slot])
            drain(z_buf.at[view, slot], z_s.at[view, slot])
    drain(soft_ybuf, soft_s.at[0])
    drain(soft_zbuf, soft_s.at[1])
    drain(loss_ybuf, loss_s.at[0])
    drain(loss_zbuf, loss_s.at[1])
    drain(loss_xbuf, loss_s.at[2])
    drain(sr_ref, ss_s)
    drain(xo_ref, xo_s)
    drain(xr_ref, xs_s)


def solution(mesh):
    ndp, nproto = mesh.shape["dp"], mesh.shape["proto"]
    nx, nz = ndp // CORES, DEPTH
    ny = nproto // nz

    def local(first, second, protos, pairing):
        fr, width = first.shape
        pr = protos.shape[0]
        frames = fr * nproto
        cols = pr * ndp
        fd = frames // 128
        ct = cols // 128
        sem = pltpu.SemaphoreType.DMA
        sizes = (nx, ny, nz, fr, width, pr)
        vmem = pltpu.VMEM
        grad, loss = pl.pallas_call(
            functools.partial(kernel, sizes),
            out_shape=(
                jax.ShapeDtypeStruct((pr, width), F32),
                jax.ShapeDtypeStruct((1, 1), F32),
            ),
            in_specs=[pl.BlockSpec(memory_space=pltpu.VMEM)] * 4,
            out_specs=(
                pl.BlockSpec(memory_space=pltpu.VMEM),
                pl.BlockSpec(memory_space=pltpu.SMEM),
            ),
            scratch_shapes=[
                vmem((nz, ny, 2, fr, width), BF16),
                vmem((frames, width), BF16),
                vmem((ndp, pr, width), BF16),
                vmem((frames, frames), BF16),
                vmem((2, width, frames), BF16),
                vmem((2, frames, cols), F32),
                vmem((frames, cols), F32),
                vmem((2, frames, 128), F32),
                vmem((2, frames, 128), F32),
                vmem((2, frames, 128), F32),
                vmem((2, frames, 128), F32),
                vmem((2, 8, cols), F32),
                vmem((2, ct, 128), F32),
                vmem((4, fd, 128), F32),
                vmem((2, fd, 128), F32),
                vmem((2, fd, 128), F32),
                vmem((2, frames, pr), BF16),
                vmem((nx, width, pr), F32),
                vmem((2, 2, ct, 128), F32),
                vmem((2, 2, ndp - 1, ct, 128), F32),
                vmem((2, 2, fd, 128), F32),
                vmem((2, 2, ny - 1, fd, 128), F32),
                vmem((2, 2, fd, 128), F32),
                vmem((2, 2, nz - 1, fd, 128), F32),
                vmem((2 * fd, 128), F32),
                vmem((ny - 1, 2 * fd, 128), F32),
                vmem((2 * fd, 128), F32),
                vmem((nz - 1, 2 * fd, 128), F32),
                vmem((3, fd, 128), F32),
                vmem((ny - 1, fd, 128), F32),
                vmem((nz - 1, fd, 128), F32),
                vmem((ndp - 1, fd, 128), F32),
                vmem((nx, width, pr), BF16),
                vmem((nx, width, pr), BF16),
                vmem((nx - 1, width, pr), BF16),
                vmem((2, width, pr), BF16),
                vmem((2, width // 2, pr), BF16),
                sem, sem((ny - 1,)),
                sem((2,)), sem((2, nz // 2, ny)),
                sem, sem,
                sem, sem((nz,)),
                sem, sem((2, 2)), sem((2,)),
                sem, sem,
                sem((2, 2)), sem((2, 2)),
                sem((2, 2)), sem((2, 2)),
                sem((2, 2)), sem((2, 2)),
                sem((2,)), sem((2,)),
                sem((3,)), sem((3,)),
                sem, sem((nx,)),
                sem, sem,
                sem, sem((2,)),
            ],
            compiler_params=pltpu.CompilerParams(
                collective_id=0, has_side_effects=True, vmem_limit_bytes=56 * 2**20
            ),
        )(first, second, protos, pairing.reshape(fd, 128))
        return grad, loss[0, 0]

    return jax.shard_map(
        local,
        mesh=mesh,
        in_specs=(
            P(("dp", "proto"), None),
            P(("dp", "proto"), None),
            P(("dp", "proto"), None),
            P("dp"),
        ),
        out_specs=(P(("dp", "proto"), None), P()),
        check_vma=False,
    )
```

time: 103 us -> 96.5 us (0.937)
  Pallas kernels: 98.9 us -> 92.1 us
    pallas_call x1, Pallas kernels: 98.9 us -> 92.1 us  [local(): pl.pallas_call(functools.partial(kernel, sizes), out_shape=(jax.ShapeDtyp...]
where the time goes in v3:
time: 96.5 us; the launch traced here: 96.3 us
  Pallas kernels  92.1 us (95%)
  between operations  2.34 us (2%)
  local copies, waits for them, and re-layouts  1.87 us (2%)
    pallas_call x1, Pallas kernels, local(): pl.pallas_call(functools.partial(kernel, sizes), out_shape=(jax.ShapeDtyp...  92.1 us

profile of v3, /device:TPU:1, one launch (start us, length us, event | category | flops | bytes accessed | tf_op | source)
XLA Modules:
  0.0 96.3 jit_solution(7272888243512614649)
XLA Ops:
  0.6 92.1 %shard_map.59 = (f32[256,512]{1,0:T(8,128)}, f32[1,1]{1,0:T(1,128)}) custom-call(bf16[32,512]{1,0:T(8,128)(2,1)} %first_ref.1, bf16[32,512]{1,0:T(8,128)(2,1)} %second_ref.1, f32[256,512]{1,0:T(8,128)} %protos_ref.1, s32[8,128]{1,0:T(8,128)} %bitcast.2), custom_call_target="tpu_custom_call" | custom-call | tf_op jit(solution)/shard_map/pallas_call | solution.py:747
  92.7 1.9 %copy.8 = f32[256,512]{1,0:T(8,128)} copy(f32[256,512]{1,0:T(8,128)} %get-tuple-element.8) | data formatting | bytes 1048576

commit v4 on v3

--- a/solution.py
+++ b/solution.py
@@ -52,6 +52,11 @@
     pair_ref,
     grad_ref,
     loss_ref,
+    first_in,
+    second_in,
+    protos_in,
+    pair_in,
+    grad_out,
     v_ref,
     partner_ref,
     p_ref,
@@ -74,8 +79,6 @@
     dp_buf,
     y_src,
     y_buf,
-    z_src,
-    z_buf,
     soft_src,
     soft_ybuf,
     soft_mid,
@@ -89,6 +92,8 @@
     xs_ref,
     xr_ref,
     xo_ref,
+    in_s,
+    out_s,
     ay_s,
     ay_r,
     zr_s,
@@ -106,8 +111,6 @@
     dp_r,
     y_s,
     y_r,
-    z_s,
-    z_r,
     soft_s,
     soft_r,
     loss_s,
@@ -152,6 +155,10 @@
     xs = [at(dx=d) for d in range(1, nx)]
     ys = [at(dy=d) for d in range(1, ny)]
     zs = [at(dz=d) for d in range(1, nz)]
+    around = lambda d, n: min(d, n - d)
+    offsets = [(d, e) for d in range(ny) for e in range(nz) if d or e]
+    offsets.sort(key=lambda o: -around(o[0], ny) - around(o[1], nz))
+    yzs = [at(dy=d, dz=e) for d, e in offsets]
     dps = [at(dx=d, dc=e) for d in range(nx) for e in range(CORES) if d or e]
 
     last = nz // 2
@@ -212,15 +219,31 @@
         drain(piece, po_r.at[part])
         send(piece, piece, ps_s, ps_r, sib)
 
+    loads = [
+        pltpu.make_async_copy(source, target, in_s.at[i])
+        for i, (source, target) in enumerate(
+            (
+                (first_ref, first_in),
+                (second_ref, second_in),
+                (protos_ref, protos_in),
+                (pair_ref, pair_in),
+            )
+        )
+    ]
+    for load in loads:
+        load.start()
+
     barrier = pltpu.get_barrier_semaphore()
-    for device in dps + ys + zs:
+    for device in dps + yzs:
         pl.semaphore_signal(
             barrier, inc=1, device_id=device, device_id_type=pl.DeviceIdType.MESH
         )
-    v_ref[z, y, 0] = unit_rows(first_ref[...])
-    v_ref[z, y, 1] = unit_rows(second_ref[...])
-    p_ref[dp] = unit_rows(protos_ref[...])
-    pl.semaphore_wait(barrier, len(dps) + len(ys) + len(zs))
+    for load in loads:
+        load.wait()
+    v_ref[z, y, 0] = unit_rows(first_in[...])
+    v_ref[z, y, 1] = unit_rows(second_in[...])
+    p_ref[dp] = unit_rows(protos_in[...])
+    pl.semaphore_wait(barrier, len(dps) + len(yzs))
 
     for j, device in enumerate(ys):
         send(chunk(0), chunk(0), ay_s, ay_r.at[j], device)
@@ -235,7 +258,7 @@
             send(piece, piece, px_s, where, xs[0 if way == 0 else nx - 2])
     send(p_ref.at[dp], p_ref.at[dp], ps_s, ps_r, sib)
 
-    pair = pair_ref[...]
+    pair = pair_in[...]
     where = (pair % (nz * fr) // fr) * group + (pair // (nz * fr)) * fr + pair % fr
     where = where.astype(F32)
     for b in range(fdense):
@@ -365,7 +388,7 @@
             total = total + dp_buf[view, slot, j]
         return total
 
-    def y_start(view, it):
+    def yz_start(view, it):
         slot = it % 2
 
         @pl.when(it >= 2)
@@ -373,7 +396,7 @@
             drain(y_buf.at[view, slot], y_s.at[view, slot])
 
         y_src[view, slot] = row_ref[view]
-        for j, device in enumerate(ys):
+        for j, device in enumerate(yzs):
             send(
                 y_src.at[view, slot],
                 y_buf.at[view, slot, j],
@@ -382,33 +405,12 @@
                 device,
             )
 
-    def y_wait(view, it):
+    def yz_wait(view, it):
         slot = it % 2
         drain(y_buf.at[view, slot], y_r.at[view, slot])
         total = y_src[view, slot]
-        for j in range(len(ys)):
+        for j in range(len(yzs)):
             total = total + y_buf[view, slot, j]
-
-        @pl.when(it >= 2)
-        def _():
-            drain(z_buf.at[view, slot], z_s.at[view, slot])
-
-        z_src[view, slot] = total
-        for j, device in enumerate(zs):
-            send(
-                z_src.at[view, slot],
-                z_buf.at[view, slot, j],
-                z_s.at[view, slot],
-                z_r.at[view, slot],
-                device,
-            )
-
-    def z_wait(view, it):
-        slot = it % 2
-        drain(z_buf.at[view, slot], z_r.at[view, slot])
-        total = z_src[view, slot]
-        for j in range(len(zs)):
-            total = total + z_buf[view, slot, j]
         return total
 
     def column_totals(view):
@@ -562,21 +564,14 @@
         for view in (1, 0):
             c_ref[view] = 1.0 / dp_wait(view, it)
             frame_sums(view)
-            y_start(view, it)
+            yz_start(view, it)
 
         @pl.when(it == 0)
         def _():
-            align_kernel(0, pieces // 2)
+            align_kernel(0, pieces)
             soft_rows()
-
-        for view in (1, 0):
-            y_wait(view, it)
-
-        @pl.when(it == 0)
-        def _():
             for j, device in enumerate(zs):
                 send(soft_mid, soft_zbuf.at[j], soft_s.at[1], soft_r.at[1], device)
-            align_kernel(pieces // 2, pieces - pieces // 2)
 
         @pl.when(it == 1)
         def _():
@@ -587,7 +582,7 @@
             cross_sums()
 
         for view in (1, 0):
-            r_ref[view] = 1.0 / z_wait(view, it)
+            r_ref[view] = 1.0 / yz_wait(view, it)
 
             @pl.when(it < ITERS - 1)
             def _(view=view):
@@ -697,16 +692,24 @@
     lax.fori_loop(0, 2 * nx, scatter, 0)
     loss_step(1, loss_zbuf, loss_xbuf, dps)
     drain(xr_ref, xs_r)
+    stores = []
     for i in range(width // 128):
+        rows = slice(i * 128, (i + 1) * 128)
         for t in range(tiles_pr):
-            rows, cols = slice(i * 128, (i + 1) * 128), slice(t * 128, (t + 1) * 128)
+            cols = slice(t * 128, (t + 1) * 128)
             total = g_ref[3, rows, cols] + sr_ref[3, rows, cols].astype(F32)
             for j in range(2):
                 total = total + xr_ref[j, rows, cols].astype(F32)
-            grad_ref[cols, rows] = total.T
+            grad_out[cols, rows] = total.T
+        stores.append(
+            pltpu.make_async_copy(grad_out.at[:, rows], grad_ref.at[:, rows], out_s.at[i])
+        )
+        stores[i].start()
     total = loss_step(2, loss_xbuf, None, None)
     loss_ref[0, 0] = jnp.sum(total) / (2.0 * frames * nx * CORES)
 
+    for store in stores:
+        store.wait()
     drain(v_ref.at[0, pl.ds(0, ny - 1)], ay_s)
     drain(v_ref.at[pl.ds(0, 2 * (last - 1)), 0], zr_s.at[0])
     drain(v_ref.at[pl.ds(0, 2 * near - split), pl.ds(0, ny - 1)], zr_s.at[1])
@@ -718,7 +721,6 @@
         for slot in range(min(2, ITERS)):
             drain(dp_buf.at[view, slot], dp_s.at[view, slot])
             drain(y_buf.at[view, slot], y_s.at[view, slot])
-            drain(z_buf.at[view, slot], z_s.at[view, slot])
     drain(soft_ybuf, soft_s.at[0])
     drain(soft_zbuf, soft_s.at[1])
     drain(loss_ybuf, loss_s.at[0])
@@ -750,12 +752,17 @@
                 jax.ShapeDtypeStruct((pr, width), F32),
                 jax.ShapeDtypeStruct((1, 1), F32),
             ),
-            in_specs=[pl.BlockSpec(memory_space=pltpu.VMEM)] * 4,
+            in_specs=[pl.BlockSpec(memory_space=pl.ANY)] * 4,
             out_specs=(
-                pl.BlockSpec(memory_space=pltpu.VMEM),
+                pl.BlockSpec(memory_space=pl.ANY),
                 pl.BlockSpec(memory_space=pltpu.SMEM),
             ),
             scratch_shapes=[
+                vmem((fr, width), BF16),
+                vmem((fr, width), BF16),
+                vmem((pr, width), F32),
+                vmem((fd, 128), jnp.int32),
+                vmem((pr, width), F32),
                 vmem((nz, ny, 2, fr, width), BF16),
                 vmem((frames, width), BF16),
                 vmem((ndp, pr, width), BF16),
@@ -777,9 +784,7 @@
                 vmem((2, 2, ct, 128), F32),
                 vmem((2, 2, ndp - 1, ct, 128), F32),
                 vmem((2, 2, fd, 128), F32),
-                vmem((2, 2, ny - 1, fd, 128), F32),
-                vmem((2, 2, fd, 128), F32),
-                vmem((2, 2, nz - 1, fd, 128), F32),
+                vmem((2, 2, nproto - 1, fd, 128), F32),
                 vmem((2 * fd, 128), F32),
                 vmem((ny - 1, 2 * fd, 128), F32),
                 vmem((2 * fd, 128), F32),
@@ -793,13 +798,13 @@
                 vmem((nx - 1, width, pr), BF16),
                 vmem((2, width, pr), BF16),
                 vmem((2, width // 2, pr), BF16),
+                sem((4,)), sem((width // 128,)),
                 sem, sem((ny - 1,)),
                 sem((2,)), sem((2, nz // 2, ny)),
                 sem, sem,
                 sem, sem((nz,)),
                 sem, sem((2, 2)), sem((2,)),
                 sem, sem,
-                sem((2, 2)), sem((2, 2)),
                 sem((2, 2)), sem((2, 2)),
                 sem((2, 2)), sem((2, 2)),
                 sem((2,)), sem((2,)),

time: 96.5 us -> 94.9 us (0.983)
  Pallas kernels: 92.1 us -> 90.5 us
    pallas_call x1, Pallas kernels: 92.1 us -> 90.5 us  [local(): pl.pallas_call(functools.partial(kernel, sizes), out_shape=(jax.ShapeDtyp...]
where the time goes in v4:
time: 94.9 us; the launch traced here: 94.7 us
  Pallas kernels  90.5 us (95%)
  between operations  2.34 us (2%)
  local copies, waits for them, and re-layouts  1.87 us (2%)
    pallas_call x1, Pallas kernels, local(): pl.pallas_call(functools.partial(kernel, sizes), out_shape=(jax.ShapeDtyp...  90.5 us

profile of v4, /device:TPU:1, one launch (start us, length us, event | category | flops | bytes accessed | tf_op | source)
XLA Modules:
  0.0 94.7 jit_solution(15939009322440432239)
XLA Ops:
  0.6 90.5 %shard_map.59 = (f32[256,512]{1,0:T(8,128)}, f32[1,1]{1,0:T(1,128)}) custom-call(bf16[32,512]{1,0:T(8,128)(2,1)} %first_ref.1, bf16[32,512]{1,0:T(8,128)(2,1)} %second_ref.1, f32[256,512]{1,0:T(8,128)} %protos_ref.1, s32[8,128]{1,0:T(8,128)} %bitcast.2), custom_call_target="tpu_custom_call" | custom-call | tf_op jit(solution)/shard_map/pallas_call | solution.py:749
  91.2 1.9 %copy.8 = f32[256,512]{1,0:T(8,128)} copy(f32[256,512]{1,0:T(8,128)} %get-tuple-element.8) | data formatting | bytes 1048576

commit v5 on v4

--- a/solution.py
+++ b/solution.py
@@ -233,8 +233,10 @@
     for load in loads:
         load.start()
 
+    greeted = [sib, xs[0], xs[nx - 2], *ys]
+    greeted += [zs[d - 1] for d in sorted({1, 2, last, nz - 2, nz - 1})]
     barrier = pltpu.get_barrier_semaphore()
-    for device in dps + yzs:
+    for device in greeted:
         pl.semaphore_signal(
             barrier, inc=1, device_id=device, device_id_type=pl.DeviceIdType.MESH
         )
@@ -243,7 +245,7 @@
     v_ref[z, y, 0] = unit_rows(first_in[...])
     v_ref[z, y, 1] = unit_rows(second_in[...])
     p_ref[dp] = unit_rows(protos_in[...])
-    pl.semaphore_wait(barrier, len(dps) + len(yzs))
+    pl.semaphore_wait(barrier, len(greeted))
 
     for j, device in enumerate(ys):
         send(chunk(0), chunk(0), ay_s, ay_r.at[j], device)
@@ -329,40 +331,6 @@
         event()
     drain(p_ref.at[pl.ds(0, nx)], ps_r)
 
-    def pair_wait(p):
-        if p == 0:
-            if near == 1:
-                for q in range(1, ny):
-                    ring_wait(1, q)
-        elif p == 1:
-            far_wait(last, far_index(last))
-        else:
-            step = last + 1 - p
-            if step <= near:
-                for q in range(1, ny):
-                    ring_wait(step, q)
-            far_wait(-step, far_index(-step))
-            far_wait(step, far_index(step))
-
-    def pair_pass(n, carry):
-        p, view = n // 2, n % 2
-        for known in range(last):
-
-            @pl.when(n == 2 * known)
-            def _(known=known):
-                pair_wait(known)
-
-        step = lax.max(1, (last + 1 - p) * lax.min(p, 1))
-        one = lax.rem(z + step, nz)
-        two = lax.rem(z + nz - step * lax.min((p - 1) * (p - 1), 1), nz)
-        block = jnp.concatenate(
-            [v_ref[b, :, view].reshape(group, width) for b in (one, two)], axis=0
-        )
-        first_pass(view, [one * group, two * group], block)
-        return carry
-
-    lax.fori_loop(0, 2 * last, pair_pass, 0)
-
     def dp_start(view, it, source):
         slot = it % 2
 
@@ -453,7 +421,46 @@
             cs_ref[view, :, t * 128 : (t + 1) * 128] = totals[t]
 
     zero = jnp.int32(0)
-    dp_start(1, zero, column_totals(1))
+
+    def pair_wait(p):
+        if p == 0:
+            if near == 1:
+                for q in range(1, ny):
+                    ring_wait(1, q)
+        elif p == 1:
+            far_wait(last, far_index(last))
+        else:
+            step = p
+            if step <= near:
+                for q in range(1, ny):
+                    ring_wait(step, q)
+            far_wait(-step, far_index(-step))
+            far_wait(step, far_index(step))
+
+    def pair_pass(n, carry):
+        p, view = n // 2, 1 - n % 2
+        for known in range(last):
+
+            @pl.when(n == 2 * known)
+            def _(known=known):
+                pair_wait(known)
+
+        opposite_pair = 1 - lax.min((p - 1) * (p - 1), 1)
+        step = p + 1 - lax.min(p, 1) + opposite_pair * (last - 1)
+        one = lax.rem(z + step, nz)
+        two = lax.rem(z + nz - step * (1 - opposite_pair), nz)
+        block = jnp.concatenate(
+            [v_ref[b, :, view].reshape(group, width) for b in (one, two)], axis=0
+        )
+        first_pass(view, [one * group, two * group], block)
+
+        @pl.when(n == 2 * last - 2)
+        def _():
+            dp_start(1, zero, column_totals(1))
+
+        return carry
+
+    lax.fori_loop(0, 2 * last, pair_pass, 0)
     dp_start(0, zero, column_totals(0))
 
     for view in range(2):

time: 94.9 us -> 92.2 us (0.972)
  Pallas kernels: 90.5 us -> 87.8 us
    pallas_call x1, Pallas kernels: 90.5 us -> 87.8 us  [local(): pl.pallas_call(functools.partial(kernel, sizes), out_shape=(jax.ShapeDtyp...]
where the time goes in v5:
time: 92.2 us; the launch traced here: 92 us
  Pallas kernels  87.8 us (95%)
  between operations  2.34 us (3%)
  local copies, waits for them, and re-layouts  1.87 us (2%)
    pallas_call x1, Pallas kernels, local(): pl.pallas_call(functools.partial(kernel, sizes), out_shape=(jax.ShapeDtyp...  87.8 us
    unnamed x1, local copies, waits for them, and re-layouts  1.87 us

profile of v5, /device:TPU:1, one launch (start us, length us, event | category | flops | bytes accessed | tf_op | source)
XLA Modules:
  0.0 92.0 jit_solution(17240081683586902547)
XLA Ops:
  0.6 87.8 %shard_map.59 = (f32[256,512]{1,0:T(8,128)}, f32[1,1]{1,0:T(1,128)}) custom-call(bf16[32,512]{1,0:T(8,128)(2,1)} %first_ref.1, bf16[32,512]{1,0:T(8,128)(2,1)} %second_ref.1, f32[256,512]{1,0:T(8,128)} %protos_ref.1, s32[8,128]{1,0:T(8,128)} %bitcast.2), custom_call_target="tpu_custom_call" | custom-call | tf_op jit(solution)/shard_map/pallas_call | solution.py:756
  88.4 1.9 %copy.8 = f32[256,512]{1,0:T(8,128)} copy(f32[256,512]{1,0:T(8,128)} %get-tuple-element.8) | data formatting | bytes 1048576

commit v6 on v5

--- a/solution.py
+++ b/solution.py
@@ -398,7 +398,7 @@
             row_ref[view, pl.ds(b, 1), :] = jnp.sum(total.T, axis=0, keepdims=True)
             return carry
 
-        lax.fori_loop(0, fdense, step, 0, unroll=min(4, fdense))
+        lax.fori_loop(0, fdense, step, 0, unroll=fdense)
 
     def proto_sums(view):
         def step(i, totals):

time: 92.2 us -> 90.7 us (0.984)
  Pallas kernels: 87.8 us -> 86.3 us
    pallas_call x1, Pallas kernels: 87.8 us -> 86.3 us  [local(): pl.pallas_call(functools.partial(kernel, sizes), out_shape=(jax.ShapeDtyp...]
where the time goes in v6:
time: 90.7 us; the launch traced here: 90.5 us
  Pallas kernels  86.3 us (95%)
  between operations  2.34 us (3%)
  local copies, waits for them, and re-layouts  1.87 us (2%)
    pallas_call x1, Pallas kernels, local(): pl.pallas_call(functools.partial(kernel, sizes), out_shape=(jax.ShapeDtyp...  86.3 us
    unnamed x1, local copies, waits for them, and re-layouts  1.87 us

profile of v6, /device:TPU:1, one launch (start us, length us, event | category | flops | bytes accessed | tf_op | source)
XLA Modules:
  0.0 90.5 jit_solution(6646894801780268680)
XLA Ops:
  0.6 86.3 %shard_map.59 = (f32[256,512]{1,0:T(8,128)}, f32[1,1]{1,0:T(1,128)}) custom-call(bf16[32,512]{1,0:T(8,128)(2,1)} %first_ref.1, bf16[32,512]{1,0:T(8,128)(2,1)} %second_ref.1, f32[256,512]{1,0:T(8,128)} %protos_ref.1, s32[8,128]{1,0:T(8,128)} %bitcast.2), custom_call_target="tpu_custom_call" | custom-call | tf_op jit(solution)/shard_map/pallas_call | solution.py:756
  86.9 1.9 %copy.8 = f32[256,512]{1,0:T(8,128)} copy(f32[256,512]{1,0:T(8,128)} %get-tuple-element.8) | data formatting | bytes 1048576

commit v7 on v6

--- a/solution.py
+++ b/solution.py
@@ -401,21 +401,21 @@
         lax.fori_loop(0, fdense, step, 0, unroll=fdense)
 
     def proto_sums(view):
-        def step(i, totals):
-            rows = pl.ds(pl.multiple_of(i * 64, 64), 64)
-            scale = rb_ref[view, rows, :]
+        def step(b, totals):
+            rows = pl.ds(pl.multiple_of(b * 128, 128), 128)
+            scale = jnp.broadcast_to(r_ref[view, pl.ds(b, 1), :], (128, 128)).T
             out = []
             for t in range(ptiles):
                 k = k_ref[view, rows, t * 128 : (t + 1) * 128]
-                out.append(totals[t] + jnp.sum((k * scale).reshape(8, 8, 128), axis=0))
+                out.append(totals[t] + jnp.sum((k * scale).reshape(16, 8, 128), axis=0))
             return tuple(out)
 
         totals = lax.fori_loop(
             0,
-            frames // 64,
+            fdense,
             step,
             tuple(jnp.zeros((8, 128), F32) for _ in range(ptiles)),
-            unroll=2,
+            unroll=fdense,
         )
         for t in range(ptiles):
             cs_ref[view, :, t * 128 : (t + 1) * 128] = totals[t]
@@ -593,7 +593,6 @@
 
             @pl.when(it < ITERS - 1)
             def _(view=view):
-                lanes_to_rows(r_ref[view], rb_ref, view, frames)
                 proto_sums(view)
                 dp_start(view, it + 1, column_totals(view))
 

time: 90.7 us -> 90.7 us (level)
  no operation moved by 1% of the time
where the time goes in v7:
time: 90.7 us; the launch traced here: 90.6 us
  Pallas kernels  86.3 us (95%)
  between operations  2.34 us (3%)
  local copies, waits for them, and re-layouts  1.87 us (2%)
    pallas_call x1, Pallas kernels, local(): pl.pallas_call(functools.partial(kernel, sizes), out_shape=(jax.ShapeDtyp...  86.3 us
    unnamed x1, local copies, waits for them, and re-layouts  1.87 us

profile of v7, /device:TPU:1, one launch (start us, length us, event | category | flops | bytes accessed | tf_op | source)
XLA Modules:
  0.0 90.6 jit_solution(4970927699828101655)
XLA Ops:
  0.6 86.3 %shard_map.59 = (f32[256,512]{1,0:T(8,128)}, f32[1,1]{1,0:T(1,128)}) custom-call(bf16[32,512]{1,0:T(8,128)(2,1)} %first_ref.1, bf16[32,512]{1,0:T(8,128)(2,1)} %second_ref.1, f32[256,512]{1,0:T(8,128)} %protos_ref.1, s32[8,128]{1,0:T(8,128)} %bitcast.2), custom_call_target="tpu_custom_call" | custom-call | tf_op jit(solution)/shard_map/pallas_call | solution.py:755
  87.0 1.9 %copy.8 = f32[256,512]{1,0:T(8,128)} copy(f32[256,512]{1,0:T(8,128)} %get-tuple-element.8) | data formatting | bytes 1048576
